TPU v7x, 32 devices: a whole 2x2x4 slice. The times are simulated.
32 devices in a mesh: seq: 8 (over y, x, core), fsdp: 4 (over z).
Axes of the slice: x: 2, y: 2, z: 4, core: 2. Of those that a mesh axis runs over, the one named last changes fastest.
Arguments:
- tokens: bfloat16 [4, 2048, 1024], P('fsdp', 'seq'), may hold values from -6 to 6
- weight_query: bfloat16 [1024, 1024], P(('seq', 'fsdp')), may hold values from -0.1875 to 0.1875
- weight_key: bfloat16 [1024, 1024], P(('seq', 'fsdp')), may hold values from -0.1875 to 0.1875
- weight_value: bfloat16 [1024, 1024], P(('seq', 'fsdp')), may hold values from -0.1875 to 0.1875
- weight_out: bfloat16 [1024, 1024], P(('seq', 'fsdp')), may hold values from -6 to 6
- weight_gate: bfloat16 [1024, 4096], P(('seq', 'fsdp')), may hold values from -0.1875 to 0.1875
- weight_up: bfloat16 [1024, 4096], P(('seq', 'fsdp')), may hold values from -0.1875 to 0.1875
- weight_down: bfloat16 [4096, 1024], P(('seq', 'fsdp')), may hold values from -0.09375 to 0.09375
- norm_attn: float32 [1024], replicated, may hold values from 0.5 to 1.5
- norm_ffn: float32 [1024], replicated, may hold values from 0.5 to 1.5
- query_gain: float32 [64], replicated, may hold values from 0.5 to 1.5
- key_gain: float32 [64], replicated, may hold values from 0.5 to 1.5
- variate_bias: float32 [2, 16], P(None, 'seq'), may hold values from -1.5 to 1.5
- variate_ids: int32 [4, 2048], P('fsdp', 'seq'), may hold values from 0 to 3
- sample_ids: int32 [4, 2048], P('fsdp', 'seq'), may hold values from 0 to 2, as said below
- time_ids: int32 [4, 2048], P('fsdp', 'seq'), may hold values from 0 to 2047
- out_grad: bfloat16 [4, 2048, 1024], P('fsdp', 'seq'), may hold values from -6 to 6
Outputs:
- layer_out: bfloat16 [4, 2048, 1024], P('fsdp', 'seq')
- in_grad: float32 [4, 2048, 1024], P('fsdp', 'seq')
- grad_weight_query: float32 [1024, 1024], P(('seq', 'fsdp'))
- grad_weight_key: float32 [1024, 1024], P(('seq', 'fsdp'))
- grad_weight_value: float32 [1024, 1024], P(('seq', 'fsdp'))
- grad_weight_out: float32 [1024, 1024], P(('seq', 'fsdp'))
- grad_weight_gate: float32 [1024, 4096], P(('seq', 'fsdp'))
- grad_weight_up: float32 [1024, 4096], P(('seq', 'fsdp'))
- grad_weight_down: float32 [4096, 1024], P(('seq', 'fsdp'))
- grad_norm_attn: float32 [1024], replicated
- grad_norm_ffn: float32 [1024], replicated
- grad_query_gain: float32 [64], replicated
- grad_key_gain: float32 [64], replicated
- grad_variate_bias: float32 [2, 16], P(None, 'seq')
Inputs may be any that keep to these rules, and one draw needn't show every extreme that they name: `sample_ids`: in each sequence the ids run 0, then 1, then 2, each run non-empty; the runs of 0 and of 2 are each shorter than 256 tokens.
All inputs are finite; a program needn't handle non-finite values.
Results may differ from a plain program's by a relative error of at most 0.025.
Values may be sent and summed in bfloat16 or wider, within the bound.
No kernel may reach another device: no remote copies, remote signals or barrier semaphores. Data moves between devices by JAX's collectives and lax.ppermute only.
A program may use at most 192 MiB of HBM per device.

v0:
```python
import math

import jax
import jax.numpy as jnp
from jax import lax
from jax.sharding import PartitionSpec as P

EPSILON = 1e-06
NEGATIVE = -1e30


def product(left_side, right_side):
    return jnp.dot(left_side, right_side, preferred_element_type=jnp.float32)


def weight_grad(left_side, right_side):
    return lax.dot_general(
        left_side, right_side, (((0,), (0,)), ((), ())), preferred_element_type=jnp.float32
    )


def back_product(left_side, right_side):
    return lax.dot_general(
        left_side, right_side, (((1,), (1,)), ((), ())), preferred_element_type=jnp.float32
    )


def rms_factor(values):
    return lax.rsqrt(jnp.mean(values * values, axis=-1, keepdims=True) + EPSILON)


def norm_back(values, factor, gain, incoming):
    weighted = incoming * gain
    grad_values = factor * weighted - values * (factor * factor * factor) * jnp.mean(
        weighted * values, axis=-1, keepdims=True
    )
    grad_gain = jnp.sum((incoming * values * factor).reshape(-1, values.shape[-1]), axis=0)
    return (grad_values, grad_gain)


def rotation(positions, head_size):
    half_size = head_size // 2
    frequency = 10000.0 ** (-2.0 * jnp.arange(half_size).astype(jnp.float32) / head_size)
    angles = positions.reshape(-1).astype(jnp.float32)[:, None] * frequency[None, :]
    return (jnp.cos(angles)[:, None, :], jnp.sin(angles)[:, None, :])


def rotate(values, cosine_table, sine_table, direction):
    half_size = values.shape[-1] // 2
    first_half = values[..., :half_size]
    second_half = values[..., half_size:]
    return jnp.concatenate(
        [
            first_half * cosine_table - direction * second_half * sine_table,
            direction * first_half * sine_table + second_half * cosine_table,
        ],
        axis=-1,
    )


def block_scores(
    query_block, key_rows, query_variate, key_variate, query_sample, key_sample, bias_pair, factor
):
    scores = (
        jnp.einsum("qhd,khd->hqk", query_block, key_rows, preferred_element_type=jnp.float32)
        * factor
    )
    same_variate = query_variate[:, None] == key_variate[None, :]
    scores = scores + jnp.where(
        same_variate[None], bias_pair[0][:, None, None], bias_pair[1][:, None, None]
    )
    allowed = (query_sample[:, None] == key_sample[None, :])[None]
    return (scores, same_variate, allowed)


def attend_forward(queries, key_rows, value_rows, variates, samples, bias_pair, block_rows):
    length, heads_dev, head_size = queries.shape
    factor = head_size ** (-0.5)
    block_count = length // block_rows

    def one_block(pieces):
        query_block, query_variate, query_sample = pieces
        scores, same_variate, allowed = block_scores(
            query_block, key_rows, query_variate, variates, query_sample, samples, bias_pair, factor
        )
        scores = jnp.where(allowed, scores, NEGATIVE)
        row_peak = jnp.max(scores, axis=-1, keepdims=True)
        shifted = jnp.exp(scores - row_peak)
        denominator = jnp.sum(shifted, axis=-1, keepdims=True)
        weights_low = (shifted / denominator).astype(jnp.bfloat16)
        mixed_block = jnp.einsum(
            "hqk,khd->qhd", weights_low, value_rows, preferred_element_type=jnp.float32
        )
        return (mixed_block.astype(jnp.bfloat16), (row_peak + jnp.log(denominator))[..., 0])

    mixed_heads, logsum = lax.map(
        one_block,
        (
            queries.reshape(block_count, block_rows, heads_dev, head_size),
            variates.reshape(block_count, block_rows),
            samples.reshape(block_count, block_rows),
        ),
    )
    return (mixed_heads.reshape(length, heads_dev, head_size), logsum)


def attend_backward(
    queries, key_rows, value_rows, grad_mixed, logsum, variates, samples, bias_pair, block_rows
):
    length, heads_dev, head_size = queries.shape
    factor = head_size ** (-0.5)
    block_count = length // block_rows
    initial = (
        jnp.zeros(key_rows.shape, jnp.float32),
        jnp.zeros(key_rows.shape, jnp.float32),
        jnp.zeros((2, heads_dev), jnp.float32),
    )

    def one_block(carry, pieces):
        grad_keys, grad_values, grad_bias = carry
        query_block, grad_block, block_logsum, query_variate, query_sample = pieces
        scores, same_variate, allowed = block_scores(
            query_block, key_rows, query_variate, variates, query_sample, samples, bias_pair, factor
        )
        weights = jnp.where(allowed, jnp.exp(scores - block_logsum[..., None]), 0.0)
        grad_weights = jnp.einsum(
            "qhd,khd->hqk", grad_block, value_rows, preferred_element_type=jnp.float32
        )
        row_inner = jnp.sum(grad_weights * weights, axis=-1, keepdims=True)
        grad_scores = (weights * (grad_weights - row_inner)).astype(jnp.bfloat16)
        grad_query = (
            jnp.einsum("hqk,khd->qhd", grad_scores, key_rows, preferred_element_type=jnp.float32)
            * factor
        )
        grad_keys = (
            grad_keys
            + jnp.einsum(
                "hqk,qhd->khd", grad_scores, query_block, preferred_element_type=jnp.float32
            )
            * factor
        )
        grad_values = grad_values + jnp.einsum(
            "hqk,qhd->khd",
            weights.astype(jnp.bfloat16),
            grad_block,
            preferred_element_type=jnp.float32,
        )
        rounded = grad_scores.astype(jnp.float32)
        same_sum = jnp.sum(jnp.where(same_variate[None], rounded, 0.0), axis=(1, 2))
        other_sum = jnp.sum(jnp.where(same_variate[None], 0.0, rounded), axis=(1, 2))
        grad_bias = grad_bias + jnp.stack([same_sum, other_sum])
        return ((grad_keys, grad_values, grad_bias), grad_query.astype(jnp.bfloat16))

    (grad_keys, grad_values, grad_bias), grad_queries = lax.scan(
        one_block,
        initial,
        (
            queries.reshape(block_count, block_rows, heads_dev, head_size),
            grad_mixed.reshape(block_count, block_rows, heads_dev, head_size),
            logsum,
            variates.reshape(block_count, block_rows),
            samples.reshape(block_count, block_rows),
        ),
    )
    return (
        grad_queries.reshape(length, heads_dev, head_size),
        grad_keys.astype(jnp.bfloat16),
        grad_values.astype(jnp.bfloat16),
        grad_bias,
    )


def body(
    tokens,
    weight_query,
    weight_key,
    weight_value,
    weight_out,
    weight_gate,
    weight_up,
    weight_down,
    norm_attn,
    norm_ffn,
    query_gain,
    key_gain,
    variate_bias,
    variate_ids,
    sample_ids,
    time_ids,
    out_grad,
):
    seq_count = lax.axis_size("seq")
    batch_size, rows_dev, model_width = tokens.shape
    heads_dev = variate_bias.shape[1]
    head_size = query_gain.shape[0]
    heads_all = heads_dev * seq_count
    length = rows_dev * seq_count
    block_rows = math.gcd(length, 512)
    token_rows = batch_size * rows_dev
    full_variates, full_samples = (
        lax.all_gather(variate_ids, "seq", axis=1, tiled=True),
        lax.all_gather(sample_ids, "seq", axis=1, tiled=True),
    )
    shards = (
        weight_query,
        weight_key,
        weight_value,
        weight_out,
        weight_gate,
        weight_up,
        weight_down,
    )
    full_query, full_key, full_value, full_out, full_gate, full_up, full_down = (
        lax.all_gather(weight_query, ("seq", "fsdp"), axis=0, tiled=True),
        lax.all_gather(weight_key, ("seq", "fsdp"), axis=0, tiled=True),
        lax.all_gather(weight_value, ("seq", "fsdp"), axis=0, tiled=True),
        lax.all_gather(weight_out, ("seq", "fsdp"), axis=0, tiled=True),
        lax.all_gather(weight_gate, ("seq", "fsdp"), axis=0, tiled=True),
        lax.all_gather(weight_up, ("seq", "fsdp"), axis=0, tiled=True),
        lax.all_gather(weight_down, ("seq", "fsdp"), axis=0, tiled=True),
    )
    hidden_in = tokens.astype(jnp.float32).reshape(token_rows, model_width)
    first_factor = rms_factor(hidden_in)
    normed_in = (hidden_in * first_factor * norm_attn).astype(jnp.bfloat16)
    query_lin = product(normed_in, full_query).reshape(token_rows, heads_all, head_size)
    key_lin = product(normed_in, full_key).reshape(token_rows, heads_all, head_size)
    value_rows = product(normed_in, full_value).astype(jnp.bfloat16)
    query_factor = rms_factor(query_lin)
    key_factor = rms_factor(key_lin)
    cosine_table, sine_table = rotation(time_ids, head_size)
    query_rot = rotate(query_lin * query_factor * query_gain, cosine_table, sine_table, 1.0).astype(
        jnp.bfloat16
    )
    key_rot = rotate(key_lin * key_factor * key_gain, cosine_table, sine_table, 1.0).astype(
        jnp.bfloat16
    )

    def to_heads(values):
        return values.reshape(batch_size, rows_dev, seq_count, heads_dev, head_size)

    query_heads, key_heads, value_heads = (
        lax.all_to_all(to_heads(query_rot), "seq", split_axis=2, concat_axis=1, tiled=True),
        lax.all_to_all(to_heads(key_rot), "seq", split_axis=2, concat_axis=1, tiled=True),
        lax.all_to_all(to_heads(value_rows), "seq", split_axis=2, concat_axis=1, tiled=True),
    )

    def forward_one(pieces):
        queries, key_rows, value_block, variates, samples = pieces
        return attend_forward(
            queries[:, 0],
            key_rows[:, 0],
            value_block[:, 0],
            variates,
            samples,
            variate_bias,
            block_rows,
        )

    mixed_heads, logsum = lax.map(
        forward_one, (query_heads, key_heads, value_heads, full_variates, full_samples)
    )
    mixed_tokens = lax.all_to_all(
        mixed_heads[:, :, None], "seq", split_axis=1, concat_axis=2, tiled=True
    )
    mixed_rows = mixed_tokens.reshape(token_rows, model_width)
    middle = hidden_in + product(mixed_rows, full_out)
    second_factor = rms_factor(middle)
    normed_mid = (middle * second_factor * norm_ffn).astype(jnp.bfloat16)
    gate_lin = product(normed_mid, full_gate)
    up_lin = product(normed_mid, full_up)
    sigmoid_gate = jax.nn.sigmoid(gate_lin)
    inner_rows = (gate_lin * sigmoid_gate * up_lin).astype(jnp.bfloat16)
    layer_out = (middle + product(inner_rows, full_down)).astype(jnp.bfloat16).reshape(tokens.shape)
    full_query, full_key, full_value, full_out, full_gate, full_up, full_down = (
        lax.all_gather(shards[0], ("seq", "fsdp"), axis=0, tiled=True),
        lax.all_gather(shards[1], ("seq", "fsdp"), axis=0, tiled=True),
        lax.all_gather(shards[2], ("seq", "fsdp"), axis=0, tiled=True),
        lax.all_gather(shards[3], ("seq", "fsdp"), axis=0, tiled=True),
        lax.all_gather(shards[4], ("seq", "fsdp"), axis=0, tiled=True),
        lax.all_gather(shards[5], ("seq", "fsdp"), axis=0, tiled=True),
        lax.all_gather(shards[6], ("seq", "fsdp"), axis=0, tiled=True),
    )
    cotangent = out_grad.astype(jnp.float32).reshape(token_rows, model_width)
    cotangent_low = out_grad.reshape(token_rows, model_width)
    grad_down = weight_grad(inner_rows, cotangent_low)
    grad_inner = back_product(cotangent_low, full_down)
    grad_gate = (
        grad_inner * up_lin * sigmoid_gate * (1.0 + gate_lin * (1.0 - sigmoid_gate))
    ).astype(jnp.bfloat16)
    grad_up = (grad_inner * gate_lin * sigmoid_gate).astype(jnp.bfloat16)
    grad_wgate = weight_grad(normed_mid, grad_gate)
    grad_wup = weight_grad(normed_mid, grad_up)
    grad_normed_mid = back_product(grad_gate, full_gate) + back_product(grad_up, full_up)
    grad_middle_norm, grad_norm_ffn = norm_back(middle, second_factor, norm_ffn, grad_normed_mid)
    grad_middle = cotangent + grad_middle_norm
    grad_branch = grad_middle.astype(jnp.bfloat16)
    grad_wout = weight_grad(mixed_rows, grad_branch)
    grad_mixed = back_product(grad_branch, full_out).astype(jnp.bfloat16)
    grad_heads = lax.all_to_all(
        to_heads(grad_mixed), "seq", split_axis=2, concat_axis=1, tiled=True
    )

    def backward_one(pieces):
        queries, key_rows, value_block, grad_block, block_logsum, variates, samples = pieces
        return attend_backward(
            queries[:, 0],
            key_rows[:, 0],
            value_block[:, 0],
            grad_block[:, 0],
            block_logsum,
            variates,
            samples,
            variate_bias,
            block_rows,
        )

    grad_query_heads, grad_key_heads, grad_value_heads, bias_parts = lax.map(
        backward_one,
        (query_heads, key_heads, value_heads, grad_heads, logsum, full_variates, full_samples),
    )
    grad_bias = jnp.sum(bias_parts, axis=0)
    grad_query_tok, grad_key_tok, grad_value_tok = (
        lax.all_to_all(
            grad_query_heads[:, :, None], "seq", split_axis=1, concat_axis=2, tiled=True
        ),
        lax.all_to_all(grad_key_heads[:, :, None], "seq", split_axis=1, concat_axis=2, tiled=True),
        lax.all_to_all(
            grad_value_heads[:, :, None], "seq", split_axis=1, concat_axis=2, tiled=True
        ),
    )
    grad_query_rot = grad_query_tok.reshape(token_rows, heads_all, head_size).astype(jnp.float32)
    grad_key_rot = grad_key_tok.reshape(token_rows, heads_all, head_size).astype(jnp.float32)
    grad_query_normed = rotate(grad_query_rot, cosine_table, sine_table, -1.0)
    grad_key_normed = rotate(grad_key_rot, cosine_table, sine_table, -1.0)
    grad_query_lin, grad_qgain = norm_back(query_lin, query_factor, query_gain, grad_query_normed)
    grad_key_lin, grad_kgain = norm_back(key_lin, key_factor, key_gain, grad_key_normed)
    grad_query_lin = grad_query_lin.reshape(token_rows, model_width).astype(jnp.bfloat16)
    grad_key_lin = grad_key_lin.reshape(token_rows, model_width).astype(jnp.bfloat16)
    grad_value_lin = grad_value_tok.reshape(token_rows, model_width)
    grad_wquery = weight_grad(normed_in, grad_query_lin)
    grad_wkey = weight_grad(normed_in, grad_key_lin)
    grad_wvalue = weight_grad(normed_in, grad_value_lin)
    grad_normed_in = (
        back_product(grad_query_lin, full_query)
        + back_product(grad_key_lin, full_key)
        + back_product(grad_value_lin, full_value)
    )
    grad_in_norm, grad_norm_attn = norm_back(hidden_in, first_factor, norm_attn, grad_normed_in)
    in_grad = (grad_middle + grad_in_norm).reshape(tokens.shape)
    sum_query, sum_key, sum_value, sum_out, sum_gate, sum_up, sum_down = (
        lax.psum_scatter(grad_wquery, ("seq", "fsdp"), scatter_dimension=0, tiled=True),
        lax.psum_scatter(grad_wkey, ("seq", "fsdp"), scatter_dimension=0, tiled=True),
        lax.psum_scatter(grad_wvalue, ("seq", "fsdp"), scatter_dimension=0, tiled=True),
        lax.psum_scatter(grad_wout, ("seq", "fsdp"), scatter_dimension=0, tiled=True),
        lax.psum_scatter(grad_wgate, ("seq", "fsdp"), scatter_dimension=0, tiled=True),
        lax.psum_scatter(grad_wup, ("seq", "fsdp"), scatter_dimension=0, tiled=True),
        lax.psum_scatter(grad_down, ("seq", "fsdp"), scatter_dimension=0, tiled=True),
    )
    gain_grads = lax.psum((grad_norm_attn, grad_norm_ffn, grad_qgain, grad_kgain), ("seq", "fsdp"))
    bias_total = lax.psum(grad_bias, "fsdp")
    return (
        layer_out,
        in_grad,
        sum_query,
        sum_key,
        sum_value,
        sum_out,
        sum_gate,
        sum_up,
        sum_down,
        gain_grads[0],
        gain_grads[1],
        gain_grads[2],
        gain_grads[3],
        bias_total,
    )


def solution(mesh):
    placed = (
        P("fsdp", "seq", None),
        P(("seq", "fsdp"), None),
        P(("seq", "fsdp"), None),
        P(("seq", "fsdp"), None),
        P(("seq", "fsdp"), None),
        P(("seq", "fsdp"), None),
        P(("seq", "fsdp"), None),
        P(("seq", "fsdp"), None),
        P(),
        P(),
        P(),
        P(),
        P(None, "seq"),
        P("fsdp", "seq"),
        P("fsdp", "seq"),
        P("fsdp", "seq"),
        P("fsdp", "seq", None),
    )
    return jax.shard_map(
        body,
        mesh=mesh,
        in_specs=placed,
        out_specs=(
            P("fsdp", "seq", None),
            P("fsdp", "seq", None),
            P(("seq", "fsdp"), None),
            P(("seq", "fsdp"), None),
            P(("seq", "fsdp"), None),
            P(("seq", "fsdp"), None),
            P(("seq", "fsdp"), None),
            P(("seq", "fsdp"), None),
            P(("seq", "fsdp"), None),
            P(),
            P(),
            P(),
            P(),
            P(None, "seq"),
        ),
        check_vma=False,
    )
```

profile of v0, /device:TPU:0, one launch (start us, length us, event | category | flops | bytes accessed | tf_op | source)
XLA Modules:
  0.0 2228.6 jit_solution(4059883344865694305)
XLA Ops:
  14.4 55.7 %all-gather.10.cloned.1.call-done = bf16[1024,1024]{1,0:T(8,128)(2,1)} async-done(((bf16[32,1024]{1,0:T(8,128)(2,1)}), bf16[1024,1024]{1,0:T(8,128)(2,1)}) %all-gather.10.cloned.1.call-update) | async-done | bytes 2097168 | tf_op jit(solution)/shard_map/all_gather | solution.py:215
  74.1 54.3 %all-gather.8.cloned.1.call-done = bf16[1024,1024]{1,0:T(8,128)(2,1)} async-done(((bf16[32,1024]{1,0:T(8,128)(2,1)}), bf16[1024,1024]{1,0:T(8,128)(2,1)}) %all-gather.8.cloned.1.call-update) | async-done | bytes 2097168 | tf_op jit(solution)/shard_map/all_gather | solution.py:214
  143.5 8.8 all-to-all-done.1
  155.9 32.5 %all-gather.12.cloned.1.call-done = bf16[1024,1024]{1,0:T(8,128)(2,1)} async-done(((bf16[32,1024]{1,0:T(8,128)(2,1)}), bf16[1024,1024]{1,0:T(8,128)(2,1)}) %all-gather.12.cloned.1.call-update) | async-done | bytes 2097168 | tf_op jit(solution)/shard_map/all_gather | solution.py:216
  196.0 12.4 all_gather.34
  220.6 48.2 %while.51 = (s32[]{:T(128)}, bf16[4,512,2,64]{1,3,2,0:T(8,128)(2,1)S(1)}, f32[4,2,512]{2,1,0:T(2,128)S(1)}, s32[4,512]{1,0:T(4,128)S(1)}, s32[2048]{0:T(1024)S(1...) while((s32[]{:T(128)}, ...), condition=%wide.region_6.7_spmd, body=%wide.region_3.6_spmd.sunk | while | flops 576781312 | bytes 34928824 | solution.py:96
  271.1 18.6 all_to_all.108
  298.0 33.1 %all-gather.16.cloned.1.call-done = bf16[1024,4096]{1,0:T(8,128)(2,1)} async-done(((bf16[32,4096]{1,0:T(8,128)(2,1)}), bf16[1024,4096]{1,0:T(8,128)(2,1)}) %all-gather.16.cloned.1.call-update) | async-done | bytes 8388624 | tf_op jit(solution)/shard_map/all_gather | solution.py:218
  338.8 71.1 %all-gather.18.cloned.1.call-done = bf16[1024,4096]{1,0:T(8,128)(2,1)} async-done(((bf16[32,4096]{1,0:T(8,128)(2,1)}), bf16[1024,4096]{1,0:T(8,128)(2,1)}) %all-gather.18.cloned.1.call-update) | async-done | bytes 8388624 | tf_op jit(solution)/shard_map/all_gather | solution.py:219
  417.7 71.1 %all-gather.20.cloned.1.call-done = bf16[4096,1024]{1,0:T(8,128)(2,1)} async-done(((bf16[128,1024]{1,0:T(8,128)(2,1)}), bf16[4096,1024]{1,0:T(8,128)(2,1)}) %all-gather.20.cloned.1.call-update) | async-done | bytes 8388624 | tf_op jit(solution)/shard_map/all_gather | solution.py:220
  488.8 12.5 multiply_convert_fusion.1
  536.1 101.3 %while.52 = (s32[]{:T(128)}, f32[2048,2,64]{0,2,1:T(8,128)S(1)}, f32[2048,2,64]{0,2,1:T(8,128)S(1)}, f32[2,2]{1,0:T(2,128)S(1)}, bf16[4,512,2,64]{1,3,2,0:T(8,12...) while((s32[]{:T(128)}, f32[2048,2,64]{0,2,1:T(8,128)S(1)}, ...), condition=%wide.region_13.14_spmd.clone, body=%wide.region_9.13_spmd.clone.sunk | while | flops 1379269632 | bytes 141740912 | solution.py:154
  691.5 13.4 all_to_all.109
  709.3 9.7 fusion.88
  719.2 9.7 fusion.89
  729.9 9.7 fusion.60
  748.2 9.6 psum.39
  764.0 40.0 %all-reduce = (f32[1024]{0:T(1024)}, f32[1024]{0:T(1024)}, f32[64]{0:T(128)}, f32[64]{0:T(128)}) all-reduce(f32[1024]{0:T(1024)S(1)} %get-tuple-element.410, f32[1024]{0:T(1024)S(1)} %copy-done.47, f32[64]{0:T(128)S(1)} %get-tuple-element.406, f32[64]{0:T(128)S(1)} %get-tuple-element.404), channel_id=1, replica_groups=mesh['seq'=8,'fsdp'=4] {'seq','fsdp'}, use_global_device_ids=true, to_apply=%region_25.26 | all-reduce | flops 2176 | bytes 17408 | tf_op jit(solution)/shard_map/psum | solution.py:359
  805.3 22.8 %reduce-scatter.10.cloned.1.call-done = f32[32,1024]{1,0:T(8,128)} async-done(((f32[1024,1024]{1,0:T(8,128)}), f32[32,1024]{1,0:T(8,128)}) %reduce-scatter.10.cloned.1.call-update) | async-done | bytes 131088 | tf_op jit(solution)/shard_map/reduce_scatter | solution.py:352
  828.1 149.2 %reduce-scatter.8.cloned.1.call-done = f32[32,1024]{1,0:T(8,128)} async-done(((f32[1024,1024]{1,0:T(8,128)}), f32[32,1024]{1,0:T(8,128)}) %reduce-scatter.8.cloned.1.call-update) | async-done | bytes 131088 | tf_op jit(solution)/shard_map/reduce_scatter | solution.py:351
  977.3 149.1 %reduce-scatter.12.cloned.1.call-done = f32[32,1024]{1,0:T(8,128)} async-done(((f32[1024,1024]{1,0:T(8,128)}), f32[32,1024]{1,0:T(8,128)}) %reduce-scatter.12.cloned.1.call-update) | async-done | bytes 131088 | tf_op jit(solution)/shard_map/reduce_scatter | solution.py:353
  1126.4 365.5 %reduce-scatter.16.cloned.1.call-done = f32[32,4096]{1,0:T(8,128)} async-done(((f32[1024,4096]{1,0:T(8,128)}), f32[32,4096]{1,0:T(8,128)}) %reduce-scatter.16.cloned.1.call-update) | async-done | bytes 524304 | tf_op jit(solution)/shard_map/reduce_scatter | solution.py:355
  1491.9 365.1 %reduce-scatter.18.cloned.1.call-done = f32[32,4096]{1,0:T(8,128)} async-done(((f32[1024,4096]{1,0:T(8,128)}), f32[32,4096]{1,0:T(8,128)}) %reduce-scatter.18.cloned.1.call-update) | async-done | bytes 524304 | tf_op jit(solution)/shard_map/reduce_scatter | solution.py:356
  1856.9 364.9 %reduce-scatter.20.cloned.1.call-done = f32[128,1024]{1,0:T(8,128)} async-done(((f32[4096,1024]{1,0:T(8,128)}), f32[128,1024]{1,0:T(8,128)}) %reduce-scatter.20.cloned.1.call-update) | async-done | bytes 524304 | tf_op jit(solution)/shard_map/reduce_scatter | solution.py:357
  (327 shorter events, 333.5 us)
Async XLA Ops:
  7.2 63.0 %all-gather.10.cloned.1.call-start = ((), (), s32[]{:S(2)}) async-start(), calls=%async_computation.16 | async-start | bytes 2162688 | tf_op jit(solution)/shard_map/all_gather | solution.py:215
  7.9 120.5 %all-gather.8.cloned.1.call-start = ((), (), s32[]{:S(2)}) async-start(), calls=%async_computation.15 | async-start | bytes 2162688 | tf_op jit(solution)/shard_map/all_gather | solution.py:214
  8.7 179.7 %all-gather.12.cloned.1.call-start = ((), (), s32[]{:S(2)}) async-start(), calls=%async_computation.17 | async-start | bytes 2162688 | tf_op jit(solution)/shard_map/all_gather | solution.py:216
  9.4 285.8 %all-gather.14.cloned.1.call-start = ((), (), s32[]{:S(2)}) async-start(), calls=%async_computation.18 | async-start | bytes 2162688 | tf_op jit(solution)/shard_map/all_gather | solution.py:217
  10.0 321.1 %all-gather.16.cloned.1.call-start = ((), (), s32[]{:S(2)}) async-start(), calls=%async_computation.19 | async-start | bytes 8650752 | tf_op jit(solution)/shard_map/all_gather | solution.py:218
  10.6 399.3 %all-gather.18.cloned.1.call-start = ((), (), s32[]{:S(2)}) async-start(), calls=%async_computation.20 | async-start | bytes 8650752 | tf_op jit(solution)/shard_map/all_gather | solution.py:219
  13.6 174.8 %copy-start.39 = (f32[256]{0:T(256)}, f32[256]{0:T(256)S(1)}, u32[]{:S(2)}) copy-start(f32[256]{0:T(256)S(1)} %get-tuple-element.504) | copy-start | bytes 3076
  14.4 123.6 %copy-start.27 = (f32[256,32]{0,1:T(8,128)}, f32[256,32]{0,1:T(8,128)S(1)}, u32[]{:S(2)}) copy-start(f32[256,32]{0,1:T(8,128)S(1)} %get-tuple-element.502) | copy-start | bytes 98308
  139.2 13.2 all-to-all-start.1
  152.4 39.4 %all-to-all-start = ((bf16[1,256,8,2,64]{1,4,3,0,2:T(8,128)(2,1)}), bf16[1,256,8,2,64]{1,4,3,0,2:T(8,128)(2,1)S(1)}, u32[]{:S(2)}, u32[]{:S(2)}) async-start(bf16[1,256,8,2,64]{1,4,3,0,2:T(8,128)(2,1)} %pad_maximum_fusion.2), calls=%async_computation | async-start | bytes 1048576 | tf_op jit(solution)/shard_map/all_to_all | solution.py:242
  191.7 28.3 %all-to-all-start.2 = ((bf16[1,256,8,2,64]{1,4,3,0,2:T(8,128)(2,1)}), bf16[1,256,8,2,64]{1,4,3,0,2:T(8,128)(2,1)S(1)}, u32[]{:S(2)}, u32[]{:S(2)}) async-start(bf16[1,256,8,2,64]{1,4,3,0,2:T(8,128)(2,1)} %bitcast.31), calls=%async_computation.2 | async-start | bytes 1048576 | tf_op jit(solution)/shard_map/all_to_all | solution.py:244
  195.3 293.6 %all-gather.20.cloned.1.call-start = ((), (), s32[]{:S(2)}) async-start(), calls=%async_computation.21 | async-start | bytes 8650752 | tf_op jit(solution)/shard_map/all_gather | solution.py:220
  297.8 214.2 %copy-start.6 = (f32[256,1024]{1,0:T(8,128)}, f32[256,1024]{1,0:T(8,128)S(1)}, u32[]{:S(2)}) copy-start(f32[256,1024]{1,0:T(8,128)S(1)} %get-tuple-element.512) | copy-start | bytes 3145732
  298.0 111.9 %copy-start.13 = (bf16[256,1024]{1,0:T(8,128)(2,1)}, bf16[256,1024]{1,0:T(8,128)(2,1)S(1)}, u32[]{:S(2)}) copy-start(bf16[256,1024]{1,0:T(8,128)(2,1)S(1)} %multiply_convert_fusion.4) | copy-start | bytes 1572868
  515.1 13.9 all-to-all-start.4
  519.2 286.0 %reduce-scatter.14.cloned.1.call-start = ((), (), s32[]{:S(2)}) async-start(), calls=%async_computation.25 | async-start | bytes 4325376 | tf_op jit(solution)/shard_map/reduce_scatter | solution.py:354
  641.2 15.1 all-to-all-start.5
  656.4 15.1 all-to-all-start.6
  660.5 167.6 %reduce-scatter.10.cloned.1.call-start = ((), (), s32[]{:S(2)}) async-start(), calls=%async_computation.23 | async-start | bytes 4325376 | tf_op jit(solution)/shard_map/reduce_scatter | solution.py:352
  683.0 294.3 %reduce-scatter.8.cloned.1.call-start = ((), (), s32[]{:S(2)}) async-start(), calls=%async_computation.22 | async-start | bytes 4325376 | tf_op jit(solution)/shard_map/reduce_scatter | solution.py:351
  689.1 437.3 %reduce-scatter.12.cloned.1.call-start = ((), (), s32[]{:S(2)}) async-start(), calls=%async_computation.24 | async-start | bytes 4325376 | tf_op jit(solution)/shard_map/reduce_scatter | solution.py:353
  709.3 782.6 %reduce-scatter.16.cloned.1.call-start = ((), (), s32[]{:S(2)}) async-start(), calls=%async_computation.26 | async-start | bytes 17301504 | tf_op jit(solution)/shard_map/reduce_scatter | solution.py:355
  719.1 1137.8 %reduce-scatter.18.cloned.1.call-start = ((), (), s32[]{:S(2)}) async-start(), calls=%async_computation.27 | async-start | bytes 17301504 | tf_op jit(solution)/shard_map/reduce_scatter | solution.py:356
  728.9 1492.9 %reduce-scatter.20.cloned.1.call-start = ((), (), s32[]{:S(2)}) async-start(), calls=%async_computation.28 | async-start | bytes 17301504 | tf_op jit(solution)/shard_map/reduce_scatter | solution.py:357
  (53 other events, 729.6 us)
Sparse Core Ops, SparseCore 0:
  10.9 59.1 all-gather.9
  73.1 55.3 all-gather.7
  131.4 56.9 all-gather.11
  191.2 55.5 all-gather.13
  249.5 81.5 all-gather.15
  333.9 75.9 all-gather.17
  412.8 75.9 all-gather.19
  523.6 148.4 reduce-scatter.13
  683.1 144.9 reduce-scatter.9
  830.8 146.4 reduce-scatter.7
  980.1 146.2 reduce-scatter.11
  1129.1 362.7 reduce-scatter.15
  1494.7 362.1 reduce-scatter.17
  1859.6 362.1 reduce-scatter.19
where the time goes:
time: 2240 us; the launch traced here: 2230 us
  waiting for transfers between devices  1760 us (79%)
  matrix products  196 us (9%)
  blocking collectives  102 us (5%)
  other arithmetic  69.6 us (3%)
  local copies, waits for them, and re-layouts  56.7 us (3%)
  starting transfers between devices  23.6 us (1%)
    reduce_scatter x1, waiting for transfers between devices, body(): lax.psum_scatter(grad_wgate, ('seq', 'fsdp'), scatter_dimension=0, tiled=...  365 us
    reduce_scatter x1, waiting for transfers between devices, body(): lax.psum_scatter(grad_wup, ('seq', 'fsdp'), scatter_dimension=0, tiled=True)  365 us
    reduce_scatter x1, waiting for transfers between devices, body(): lax.psum_scatter(grad_down, ('seq', 'fsdp'), scatter_dimension=0, tiled=T...  365 us
    reduce_scatter x1, waiting for transfers between devices, body(): lax.psum_scatter(grad_wquery, ('seq', 'fsdp'), scatter_dimension=0, tiled...  149 us
    reduce_scatter x1, waiting for transfers between devices, body(): lax.psum_scatter(grad_wvalue, ('seq', 'fsdp'), scatter_dimension=0, tiled...  149 us
    all_gather x1, waiting for transfers between devices, body(): lax.all_gather(weight_down, ('seq', 'fsdp'), axis=0, tiled=True)  71.1 us
    all_gather x1, waiting for transfers between devices, body(): lax.all_gather(weight_up, ('seq', 'fsdp'), axis=0, tiled=True)  71.1 us
    all_gather x1, waiting for transfers between devices, body(): lax.all_gather(weight_key, ('seq', 'fsdp'), axis=0, tiled=True)  55.7 us
  transfers between devices with their start and end apart: 20, of which 16 were waited for; matrix products, arithmetic and copies ran while one was open for 13% of the time, Pallas kernels for 0%

commit v1 on v0

v1 whole, which is shorter than its diff:
```python
import functools
import math

import jax
import jax.numpy as jnp
from jax import lax
from jax.experimental import pallas as pl
from jax.experimental.pallas import tpu as pltpu
from jax.sharding import PartitionSpec as P

EPSILON = 1e-06
FAR = -1e30
LOG2E = math.log2(math.e)
WIDE = 128
ROWS_T = 160
F32 = jnp.float32
BF16 = jnp.bfloat16


def dot_nn(left, right):
    return jnp.dot(left, right, preferred_element_type=F32)


def dot_nt(left, right):
    return lax.dot_general(left, right, (((1,), (1,)), ((), ())), preferred_element_type=F32)


def dot_tn(left, right):
    return lax.dot_general(left, right, (((0,), (0,)), ((), ())), preferred_element_type=F32)


def rms_factor(values):
    return lax.rsqrt(jnp.mean(values * values, axis=-1, keepdims=True) + EPSILON)


def lanes_of(shape):
    return lax.broadcasted_iota(jnp.int32, shape, len(shape) - 1)


def head_sum(values, lane, head_size):
    low = jnp.sum(jnp.where(lane < head_size, values, 0.0), axis=-1, keepdims=True)
    high = jnp.sum(jnp.where(lane < head_size, 0.0, values), axis=-1, keepdims=True)
    return jnp.where(lane < head_size, low, high)


def partner(values, lane, head_size):
    half = head_size // 2
    up = pltpu.roll(values, WIDE - half, 1)
    down = pltpu.roll(values, half, 1)
    return jnp.where(lane % head_size < half, up, down)


def tables(lane_ref, half):
    cosine = lane_ref[0:half, :]
    sine = lane_ref[half : 2 * half, :]
    cos_rows = jnp.concatenate([cosine] * (WIDE // half), axis=0)
    sin_rows = jnp.concatenate([-sine, sine] * (WIDE // (2 * half)), axis=0)
    return cos_rows.T, sin_rows.T


def params(limit=60 * 1024 * 1024):
    return pltpu.CompilerParams(vmem_limit_bytes=limit, dimension_semantics=("arbitrary",))


def qkv_kernel(
    x_ref, w_ref, na_ref, qg_ref, kg_ref, lane_ref, bias_ref,
    nin_ref, qlin_ref, klin_ref, qa_ref, ka_ref, kt_ref, v1_ref, *, heads, head_size,
):
    half = head_size // 2
    x = x_ref[...].astype(F32)
    rows = x.shape[0]
    nin = (x * rms_factor(x) * na_ref[...]).astype(BF16)
    nin_ref[...] = nin
    lin = dot_nn(nin, w_ref[...])
    q, k, v = lin[:, :WIDE], lin[:, WIDE : 2 * WIDE], lin[:, 2 * WIDE :]
    qlin_ref[...] = q
    klin_ref[...] = k
    lane = lanes_of((rows, WIDE))
    cosine, sine = tables(lane_ref, half)

    def finish(u, gain):
        factor = lax.rsqrt(head_sum(u * u, lane, head_size) * (1.0 / head_size) + EPSILON)
        u = u * factor * gain
        return u * cosine + partner(u, lane, head_size) * sine

    q = finish(q, qg_ref[...]) * (LOG2E * head_size**-0.5)
    k = finish(k, kg_ref[...])
    row = lax.broadcasted_iota(jnp.int32, (WIDE, rows), 0)
    variate = lane_ref[2 * half : 2 * half + 1, :].astype(jnp.int32)
    sample = lane_ref[2 * half + 1 : 2 * half + 2, :].astype(jnp.int32)
    same_variate = (row % 4) == variate
    same_sample = (row - 10) == sample
    one = jnp.ones((WIDE, rows), F32)
    nil = jnp.zeros((WIDE, rows), F32)
    aug_q = jnp.where(
        row < 8,
        jnp.where(same_variate, one, nil),
        jnp.where(row < 10, one, jnp.where((row < 13) & same_sample, one, nil)),
    )
    qa_ref[...] = jnp.concatenate([q, aug_q.T], axis=1).astype(BF16)
    k_t = k.T
    for h in range(heads):
        first, second = bias_ref[0, h] * LOG2E, bias_ref[1, h] * LOG2E
        step = jnp.where(row < 8, first - second, second) * one
        high = step.astype(BF16).astype(F32)
        low = step - high
        far = jnp.where(same_sample, nil, FAR)
        plain = jnp.where(((row // 4) == 4 + h) & same_variate, one, nil)
        aug_k = jnp.where(
            row < 4,
            jnp.where(same_variate, high, nil),
            jnp.where(
                row < 8,
                jnp.where(same_variate, low, nil),
                jnp.where(
                    row == 8,
                    high,
                    jnp.where(row == 9, low, jnp.where(row < 13, far, plain)),
                ),
            ),
        )
        mine = (lane // head_size) == h
        mine_t = (row // head_size) == h
        ka_ref[h] = jnp.concatenate([jnp.where(mine, k, 0.0), aug_k.T], axis=1).astype(BF16)
        kt_ref[h] = jnp.concatenate(
            [jnp.where(mine_t, k_t, 0.0), aug_k[: ROWS_T - WIDE]], axis=0
        ).astype(BF16)
        ones_v = jnp.where((lane == h) | (lane == 2 + h), 1.0, 0.0)
        v1_ref[h] = jnp.concatenate([jnp.where(mine, v, 0.0), ones_v], axis=1).astype(BF16)


def project(x, w, norm_attn, q_gain, k_gain, lane_rows, bias, head_size, block=256):
    length, width = x.shape
    heads = bias.shape[1]
    count = lane_rows.shape[0]
    row_block = lambda cols: pl.BlockSpec((block, cols), lambda i: (i, 0))
    whole = lambda a: pl.BlockSpec(a.shape, lambda i: (0, 0))
    head_block = pl.BlockSpec((heads, block, 2 * WIDE), lambda i: (0, i, 0))
    return pl.pallas_call(
        functools.partial(qkv_kernel, heads=heads, head_size=head_size),
        grid=(length // block,),
        in_specs=[
            row_block(width), whole(w), whole(norm_attn), whole(q_gain), whole(k_gain),
            pl.BlockSpec((count, block), lambda i: (0, i)),
            pl.BlockSpec(memory_space=pltpu.SMEM),
        ],
        out_specs=[
            row_block(width), row_block(WIDE), row_block(WIDE), row_block(2 * WIDE),
            head_block, pl.BlockSpec((heads, ROWS_T, block), lambda i: (0, 0, i)), head_block,
        ],
        out_shape=[
            jax.ShapeDtypeStruct((length, width), BF16),
            jax.ShapeDtypeStruct((length, WIDE), F32),
            jax.ShapeDtypeStruct((length, WIDE), F32),
            jax.ShapeDtypeStruct((length, 2 * WIDE), BF16),
            jax.ShapeDtypeStruct((heads, length, 2 * WIDE), BF16),
            jax.ShapeDtypeStruct((heads, ROWS_T, length), BF16),
            jax.ShapeDtypeStruct((heads, length, 2 * WIDE), BF16),
        ],
        compiler_params=params(),
        cost_estimate=pl.CostEstimate(
            flops=2 * length * width * 3 * WIDE, bytes_accessed=length * width * 8, transcendentals=0
        ),
        name="project",
    )(x, w, norm_attn, q_gain, k_gain, lane_rows, bias)


def attend_kernel(qa_ref, ka_ref, v1_ref, mixed_ref, o_ref, zi_ref, *, heads, head_size, chunk):
    qa = qa_ref[...]
    length = ka_ref.shape[1]
    lane = lanes_of((qa.shape[0], WIDE))
    total = jnp.zeros((qa.shape[0], WIDE), F32)
    inverse = jnp.ones((qa.shape[0], WIDE), F32)
    for h in range(heads):
        acc = jnp.zeros((qa.shape[0], 2 * WIDE), F32)
        for c in range(length // chunk):
            part = pl.ds(c * chunk, chunk)
            e = jnp.exp2(dot_nt(qa, ka_ref[h, part, :])).astype(BF16)
            acc = acc + dot_nn(e, v1_ref[h, part, :])
        z_inv = 1.0 / acc[:, WIDE + h : WIDE + h + 1]
        total = total + acc[:, :WIDE] * z_inv
        inverse = jnp.where((lane // head_size) == h, z_inv, inverse)
    mixed_ref[...] = total.astype(BF16)
    o_ref[...] = total
    zi_ref[...] = inverse


def attend(qa, ka, v1, half, head_size, block=256, chunk=512):
    heads, length, _ = ka.shape
    rows = length // 2
    steps = rows // block
    whole = pl.BlockSpec(ka.shape, lambda i: (0, 0, 0))
    out_block = pl.BlockSpec((block, WIDE), lambda i: (i, 0))
    return pl.pallas_call(
        functools.partial(attend_kernel, heads=heads, head_size=head_size, chunk=chunk),
        grid=(steps,),
        in_specs=[
            pl.BlockSpec((block, 2 * WIDE), lambda i: (i + half * steps, 0)), whole, whole,
        ],
        out_specs=[out_block, out_block, out_block],
        out_shape=[
            jax.ShapeDtypeStruct((rows, WIDE), BF16),
            jax.ShapeDtypeStruct((rows, WIDE), F32),
            jax.ShapeDtypeStruct((rows, WIDE), F32),
        ],
        compiler_params=params(),
        cost_estimate=pl.CostEstimate(
            flops=2 * heads * rows * length * 4 * WIDE,
            bytes_accessed=length * WIDE * 16,
            transcendentals=heads * rows * length,
        ),
        name="attend",
    )(qa, ka, v1)


def attend_back_kernel(
    qa_ref, g_ref, o_ref, zi_ref, lane_ref, ka_ref, kt_ref, v1_ref,
    dq_ref, dk_ref, dv_ref, bias_ref, dk_s, dv_s, *, heads, head_size, chunk,
):
    step = pl.program_id(0)

    @pl.when(step == 0)
    def _():
        dk_s[...] = jnp.zeros_like(dk_s)
        dv_s[...] = jnp.zeros_like(dv_s)
        bias_ref[...] = jnp.zeros_like(bias_ref)

    qa = qa_ref[...]
    rows = qa.shape[0]
    length = ka_ref.shape[1]
    lane = lanes_of((rows, WIDE))
    q = qa[:, :WIDE]
    gz = (g_ref[...].astype(F32) * zi_ref[...]).astype(BF16)
    inner = gz.astype(F32) * o_ref[...]
    aug = jnp.zeros((rows, WIDE), F32)
    for h in range(heads):
        mean = -jnp.sum(
            jnp.where((lane // head_size) == h, inner, 0.0), axis=-1, keepdims=True
        ) * jnp.ones((rows, WIDE), F32)
        high = mean.astype(BF16).astype(F32)
        aug = jnp.where(lane == h, high, jnp.where(lane == 2 + h, mean - high, aug))
    ga = jnp.concatenate([gz, aug.astype(BF16)], axis=1)
    dq_t = jnp.zeros((ROWS_T, rows), F32)
    for h in range(heads):
        mine = (lane // head_size) == h
        q_h = jnp.where(mine, q, jnp.zeros_like(q))
        g_h = jnp.where(mine, gz, jnp.zeros_like(gz))
        for c in range(length // chunk):
            part = pl.ds(c * chunk, chunk)
            e = jnp.exp2(dot_nt(ka_ref[h, part, :], qa))
            ds = (e * dot_nt(v1_ref[h, part, :], ga)).astype(BF16)
            dv_s[part, :] += dot_nn(e.astype(BF16), g_h)
            dk_s[part, :] += dot_nn(ds, q_h)
            dq_t = dq_t + dot_nn(kt_ref[h, :, part], ds)
    dq_ref[...] = (dq_t[:WIDE].T * (head_size**-0.5)).astype(BF16)
    half = head_size // 2
    variate = lane_ref[2 * half : 2 * half + 1, :].astype(jnp.int32)
    columns = dq_t[WIDE + 16 : WIDE + 24]
    row = lax.broadcasted_iota(jnp.int32, columns.shape, 0)
    bias_ref[...] += jnp.concatenate(
        [jnp.where((row % 4) == variate, columns, 0.0), columns], axis=0
    )

    @pl.when(step == pl.num_programs(0) - 1)
    def _():
        dk_ref[...] = (dk_s[...] * (1.0 / LOG2E)).astype(BF16)
        dv_ref[...] = dv_s[...].astype(BF16)


def attend_back(qa, g, o, zi, lane_rows, ka, kt, v1, head_size, block=256, chunk=512):
    heads, length, _ = ka.shape
    count = lane_rows.shape[0]
    wide = pl.BlockSpec((block, WIDE), lambda i: (i, 0))
    whole = lambda a: pl.BlockSpec(a.shape, lambda i: (0,) * a.ndim)
    full = pl.BlockSpec((length, WIDE), lambda i: (0, 0))
    return pl.pallas_call(
        functools.partial(attend_back_kernel, heads=heads, head_size=head_size, chunk=chunk),
        grid=(length // block,),
        in_specs=[
            pl.BlockSpec((block, 2 * WIDE), lambda i: (i, 0)), wide, wide, wide,
            pl.BlockSpec((count, block), lambda i: (0, i)), whole(ka), whole(kt), whole(v1),
        ],
        out_specs=[wide, full, full, pl.BlockSpec((16, block), lambda i: (0, 0))],
        out_shape=[
            jax.ShapeDtypeStruct((length, WIDE), BF16),
            jax.ShapeDtypeStruct((length, WIDE), BF16),
            jax.ShapeDtypeStruct((length, WIDE), BF16),
            jax.ShapeDtypeStruct((16, block), F32),
        ],
        scratch_shapes=[pltpu.VMEM((length, WIDE), F32), pltpu.VMEM((length, WIDE), F32)],
        compiler_params=params(),
        cost_estimate=pl.CostEstimate(
            flops=2 * heads * length * length * 8 * WIDE,
            bytes_accessed=length * WIDE * 32,
            transcendentals=heads * length * length,
        ),
        name="attend_back",
    )(qa, g, o, zi, lane_rows, ka, kt, v1)


def ffn_kernel(*refs, chips, own):
    mixed = refs[: 2 * chips]
    x_ref, dout_ref, wo_ref, ws_ref, wgu_ref, wd_ref, nf_ref = refs[2 * chips : 2 * chips + 7]
    nm_ref, gnm_ref, lay_ref, inner_ref, ggu_ref, gnf_ref = refs[2 * chips + 7 : 2 * chips + 13]
    cat_own = jnp.concatenate([m[...] for m in mixed[:chips]], axis=1)
    cat_sib = jnp.concatenate([m[...] for m in mixed[chips:]], axis=1)
    hidden = wd_ref.shape[0]
    middle = x_ref[...].astype(F32) + (dot_nn(cat_own, wo_ref[...]) + dot_nn(cat_sib, ws_ref[...]))
    factor = rms_factor(middle)
    scaled = middle * factor
    nm = (scaled * nf_ref[...]).astype(BF16)
    nm_ref[...] = nm
    lin = dot_nn(nm, wgu_ref[...])
    gate, up = lin[:, :hidden], lin[:, hidden:]
    sig = jax.nn.sigmoid(gate)
    silu = gate * sig
    inner = (silu * up).astype(BF16)
    inner_ref[...] = inner
    lay_ref[...] = dot_nn(inner, wd_ref[...]).astype(BF16)
    back = dot_nt(dout_ref[...], wd_ref[...])
    g_gate = (back * up * (sig * (1.0 + gate * (1.0 - sig)))).astype(BF16)
    g_up = (back * silu).astype(BF16)
    ggu = jnp.concatenate([g_gate, g_up], axis=1)
    ggu_ref[...] = ggu
    gnm = dot_nt(ggu, wgu_ref[...])
    gnm_ref[...] = gnm.astype(BF16)

    @pl.when(pl.program_id(0) == 0)
    def _():
        gnf_ref[...] = jnp.zeros_like(gnf_ref)
        if own:
            refs[2 * chips + 13][...] = middle
            refs[2 * chips + 14][...] = jnp.concatenate([cat_own, cat_sib], axis=1)

    gnf_ref[...] += jnp.sum(gnm * scaled, axis=0, keepdims=True)


def ffn(own_parts, sib_parts, x, dout, wo_own, wo_sib, wgu, wd, norm_ffn, half, chips):
    length, width = x.shape
    rows = length // 2
    block = rows // chips
    hidden = wd.shape[0]
    own = half == 0
    base = half * chips
    row_in = pl.BlockSpec((block, width), lambda i: (i + base, 0))
    row_out = lambda cols: pl.BlockSpec((block, cols), lambda i: (i, 0))
    whole = lambda a: pl.BlockSpec(a.shape, lambda i: (0, 0))
    piece = lambda r: pl.BlockSpec((block, WIDE), lambda i: (i ^ r, 0))
    out_specs = [
        row_out(width), row_out(width), row_out(width), row_out(hidden), row_out(2 * hidden),
        pl.BlockSpec((1, width), lambda i: (0, 0)),
    ]
    out_shape = [
        jax.ShapeDtypeStruct((rows, width), BF16),
        jax.ShapeDtypeStruct((rows, width), BF16),
        jax.ShapeDtypeStruct((rows, width), BF16),
        jax.ShapeDtypeStruct((rows, hidden), BF16),
        jax.ShapeDtypeStruct((rows, 2 * hidden), BF16),
        jax.ShapeDtypeStruct((1, width), F32),
    ]
    if own:
        out_specs += [
            pl.BlockSpec((block, width), lambda i: (0, 0)),
            pl.BlockSpec((block, 2 * chips * WIDE), lambda i: (0, 0)),
        ]
        out_shape += [
            jax.ShapeDtypeStruct((block, width), F32),
            jax.ShapeDtypeStruct((block, 2 * chips * WIDE), BF16),
        ]
    return pl.pallas_call(
        functools.partial(ffn_kernel, chips=chips, own=own),
        grid=(chips,),
        in_specs=[piece(r) for r in range(chips)] * 2
        + [row_in, row_in, whole(wo_own), whole(wo_sib), whole(wgu), whole(wd), whole(norm_ffn)],
        out_specs=out_specs,
        out_shape=out_shape,
        compiler_params=params(),
        cost_estimate=pl.CostEstimate(
            flops=2 * rows * width * (2 * chips * WIDE + 6 * hidden),
            bytes_accessed=rows * width * 12,
            transcendentals=rows * hidden,
        ),
        name="ffn_half",
    )(*own_parts, *sib_parts, x, dout, wo_own, wo_sib, wgu, wd, norm_ffn)


def middle_back_kernel(*refs, chips):
    pieces = refs[:chips]
    mid_ref, dout_ref, nf_ref, wo_ref, ws_ref = refs[chips : chips + 5]
    gm_ref, gb_ref, go_ref, gs_ref = refs[chips + 5 :]
    incoming = pieces[0][...].astype(F32)
    for piece in pieces[1:]:
        incoming = incoming + piece[...].astype(F32)
    middle = mid_ref[...]
    factor = rms_factor(middle)
    weighted = incoming * nf_ref[...]
    grad = (
        dout_ref[...].astype(F32)
        + factor * weighted
        - middle * (factor * factor * factor) * jnp.mean(weighted * middle, axis=-1, keepdims=True)
    )
    gm_ref[...] = grad
    branch = grad.astype(BF16)
    gb_ref[...] = branch
    for r in range(chips):
        part = pl.ds(r * WIDE, WIDE)
        go_ref[r] = dot_nt(branch, wo_ref[part, :]).astype(BF16)
        gs_ref[r] = dot_nt(branch, ws_ref[part, :]).astype(BF16)


def middle_back(pieces, middle, dout, norm_ffn, wo_own, wo_sib):
    chips = len(pieces)
    rows, width = middle.shape
    return pl.pallas_call(
        functools.partial(middle_back_kernel, chips=chips),
        out_shape=[
            jax.ShapeDtypeStruct((rows, width), F32),
            jax.ShapeDtypeStruct((rows, width), BF16),
            jax.ShapeDtypeStruct((chips, rows, WIDE), BF16),
            jax.ShapeDtypeStruct((chips, rows, WIDE), BF16),
        ],
        compiler_params=pltpu.CompilerParams(vmem_limit_bytes=60 * 1024 * 1024),
        cost_estimate=pl.CostEstimate(
            flops=2 * rows * width * 2 * chips * WIDE, bytes_accessed=rows * width * 12, transcendentals=0
        ),
        name="middle_back",
    )(*pieces, middle, dout, norm_ffn, wo_own, wo_sib)


def input_back_kernel(*refs, chips):
    pieces = refs[:chips]
    x_ref, gm_ref, na_ref, out_ref = refs[chips:]
    incoming = pieces[0][...].astype(F32)
    for piece in pieces[1:]:
        incoming = incoming + piece[...].astype(F32)
    x = x_ref[...].astype(F32)
    factor = rms_factor(x)
    weighted = incoming * na_ref[...]
    out_ref[...] = (
        gm_ref[...]
        + factor * weighted
        - x * (factor * factor * factor) * jnp.mean(weighted * x, axis=-1, keepdims=True)
    )


def input_back(pieces, x, grad_middle, norm_attn):
    chips = len(pieces)
    return pl.pallas_call(
        functools.partial(input_back_kernel, chips=chips),
        out_shape=jax.ShapeDtypeStruct(x.shape, F32),
        compiler_params=pltpu.CompilerParams(vmem_limit_bytes=60 * 1024 * 1024),
        name="input_back",
    )(*pieces, x, grad_middle, norm_attn)


def qkv_back_kernel(
    dq_ref, dk_ref, dv_ref, qlin_ref, klin_ref, lane_ref, w_ref, x_ref, qg_ref, kg_ref,
    gni_ref, gl_ref, gain_ref, gna_ref, *, head_size,
):
    half = head_size // 2
    rows = x_ref.shape[0]
    lane = lanes_of((rows, WIDE))
    cosine, sine = tables(lane_ref, half)

    @pl.when(pl.program_id(0) == 0)
    def _():
        gain_ref[...] = jnp.zeros_like(gain_ref)
        gna_ref[...] = jnp.zeros_like(gna_ref)

    def back(grad, u, gain, at):
        grad = grad.astype(F32)
        grad = grad * cosine - partner(grad, lane, head_size) * sine
        factor = lax.rsqrt(head_sum(u * u, lane, head_size) * (1.0 / head_size) + EPSILON)
        gain_ref[at : at + 1, :] += jnp.sum(grad * u * factor, axis=0, keepdims=True)
        weighted = grad * gain
        mean = head_sum(weighted * u, lane, head_size) * (1.0 / head_size)
        return (factor * weighted - u * (factor * factor * factor) * mean).astype(BF16)

    gq = back(dq_ref[...], qlin_ref[...], qg_ref[...], 0)
    gk = back(dk_ref[...], klin_ref[...], kg_ref[...], 1)
    gl = jnp.concatenate([gq, gk, dv_ref[...]], axis=1)
    gl_ref[...] = gl
    gni = dot_nt(gl, w_ref[...])
    gni_ref[...] = gni.astype(BF16)
    x = x_ref[...].astype(F32)
    gna_ref[...] += jnp.sum(gni * x * rms_factor(x), axis=0, keepdims=True)


def qkv_back(dq, dk, dv, qlin, klin, lane_rows, w, x, q_gain, k_gain, head_size, half, block=256):
    length, width = x.shape
    count = lane_rows.shape[0]
    rows = length // 2
    base = half * (rows // block)
    row_in = lambda cols: pl.BlockSpec((block, cols), lambda i: (i + base, 0))
    row_out = lambda cols: pl.BlockSpec((block, cols), lambda i: (i, 0))
    whole = lambda a: pl.BlockSpec(a.shape, lambda i: (0, 0))
    return pl.pallas_call(
        functools.partial(qkv_back_kernel, head_size=head_size),
        grid=(rows // block,),
        in_specs=[row_in(WIDE)] * 5
        + [
            pl.BlockSpec((count, block), lambda i: (0, i + base)), whole(w), row_in(width),
            whole(q_gain), whole(k_gain),
        ],
        out_specs=[
            row_out(width), row_out(3 * WIDE),
            pl.BlockSpec((8, WIDE), lambda i: (0, 0)), pl.BlockSpec((1, width), lambda i: (0, 0)),
        ],
        out_shape=[
            jax.ShapeDtypeStruct((rows, width), BF16),
            jax.ShapeDtypeStruct((rows, 3 * WIDE), BF16),
            jax.ShapeDtypeStruct((8, WIDE), F32),
            jax.ShapeDtypeStruct((1, width), F32),
        ],
        compiler_params=params(),
        cost_estimate=pl.CostEstimate(
            flops=2 * rows * width * 3 * WIDE, bytes_accessed=rows * width * 6, transcendentals=0
        ),
        name="qkv_back",
    )(dq, dk, dv, qlin, klin, lane_rows, w, x, q_gain, k_gain)


def swap(x, seq_count, bits):
    return lax.ppermute(x, "seq", [(i, i ^ bits) for i in range(seq_count)])


def to_chips(x, seq_count):
    return [x] + [swap(x, seq_count, 2 * r) for r in range(1, seq_count // 2)]


def gather_plane(x, seq_count):
    own = jnp.concatenate(to_chips(x, seq_count), axis=0)
    return own, swap(own, seq_count, 1)


def scatter_plane(own, sib, seq_count):
    chips = seq_count // 2
    got = swap(sib, seq_count, 1)
    both = (own.astype(F32) + got.astype(F32)).astype(BF16)
    rows = both.shape[0] // chips
    parts = [both[r * rows : (r + 1) * rows] for r in range(chips)]
    return [parts[0]] + [swap(parts[r], seq_count, 2 * r) for r in range(1, chips)]


def add_up(parts):
    total = parts[0].astype(F32)
    for part in parts[1:]:
        total = total + part.astype(F32)
    return total


def body(
    tokens, weight_query, weight_key, weight_value, weight_out, weight_gate, weight_up, weight_down,
    norm_attn, norm_ffn, query_gain, key_gain, variate_bias, variate_ids, sample_ids, time_ids,
    out_grad,
):
    seq_count = lax.axis_size("seq")
    z_count = lax.axis_size("fsdp")
    chips = seq_count // 2
    _, rows_dev, width = tokens.shape
    heads = variate_bias.shape[1]
    head_size = query_gain.shape[0]
    half_size = head_size // 2
    length = rows_dev * seq_count
    half_rows = length // 2
    shard = weight_query.shape[0]
    features = heads * head_size
    hidden = weight_gate.shape[1] // seq_count
    x_own = tokens.reshape(rows_dev, width)
    dout_own = out_grad.reshape(rows_dev, width)

    lanes_pad = ((0, 0), (0, 0), (0, WIDE - features))
    columns = jnp.concatenate(
        [
            jnp.pad(w.reshape(shard, seq_count, features), lanes_pad)
            for w in (weight_query, weight_key, weight_value)
        ],
        axis=2,
    )
    columns = jnp.broadcast_to(
        columns.transpose(1, 0, 2)[:, None], (seq_count, z_count, shard, 3 * WIDE)
    ).reshape(seq_count * z_count, shard, 3 * WIDE)
    w_qkv = lax.all_to_all(
        columns, ("seq", "fsdp"), split_axis=0, concat_axis=0, tiled=True
    ).reshape(width, 3 * WIDE)
    x_halves = gather_plane(x_own, seq_count)

    down_out = lax.all_gather(
        jnp.concatenate([weight_down, weight_out], axis=0), "fsdp", axis=0, tiled=False
    )
    w_down = down_out[:, : weight_down.shape[0]].reshape(hidden, width)
    w_out_rows = down_out[:, weight_down.shape[0] :].reshape(features, width)
    if features < WIDE:
        w_out_rows = jnp.pad(w_out_rows, ((0, WIDE - features), (0, 0)))
    gate_up = jnp.concatenate(
        [w.reshape(shard, seq_count, hidden) for w in (weight_gate, weight_up)], axis=2
    ).transpose(1, 0, 2)
    gate_up = lax.all_to_all(gate_up, "seq", split_axis=0, concat_axis=0, tiled=True)
    w_gu = (
        lax.all_gather(gate_up, "fsdp", axis=0, tiled=False)
        .transpose(1, 0, 2, 3)
        .reshape(width, 2 * hidden)
    )

    ids = lax.all_gather(
        jnp.concatenate([variate_ids, sample_ids, time_ids], axis=0), "seq", axis=0, tiled=False
    )
    me = lax.axis_index("seq")
    order = jnp.concatenate([me ^ (2 * jnp.arange(chips)), me ^ (2 * jnp.arange(chips) + 1)])
    ids = ids[order].transpose(1, 0, 2).reshape(3, length).astype(F32)
    frequency = 10000.0 ** (-2.0 * jnp.arange(half_size).astype(F32) / head_size)
    angles = frequency[:, None] * ids[2][None, :]
    lane_rows = jnp.concatenate(
        [jnp.cos(angles), jnp.sin(angles), ids[:2], jnp.zeros((6, length), F32)], axis=0
    )

    gain_attn = norm_attn.reshape(1, width)
    gain_ffn = norm_ffn.reshape(1, width)
    q_gain = jnp.tile(query_gain, WIDE // head_size).reshape(1, WIDE)
    k_gain = jnp.tile(key_gain, WIDE // head_size).reshape(1, WIDE)

    x_all = jnp.concatenate(x_halves, axis=0)
    normed_in, q_lin, k_lin, q_aug, k_aug, k_trans, v_aug = project(
        x_all, w_qkv, gain_attn, q_gain, k_gain, lane_rows, variate_bias, head_size
    )
    dout_all = jnp.concatenate(gather_plane(dout_own, seq_count), axis=0)
    wo_own, wo_sib = gather_plane(w_out_rows, seq_count)

    mixed, mixed_full, z_inverse = zip(
        *[attend(q_aug, k_aug, v_aug, half, head_size) for half in (0, 1)]
    )
    own_parts = [to_chips(mixed[half], seq_count) for half in (0, 1)]
    sib_stack = [swap(jnp.concatenate(own_parts[half], axis=0), seq_count, 1) for half in (0, 1)]
    sib_parts = [
        [sib_stack[1 - half][r * half_rows : (r + 1) * half_rows] for r in range(chips)]
        for half in (0, 1)
    ]
    o_all = jnp.concatenate(mixed_full, axis=0)
    zi_all = jnp.concatenate(z_inverse, axis=0)

    far = ffn(
        own_parts[1], sib_parts[1], x_all, dout_all, wo_own, wo_sib, w_gu, w_down, gain_ffn, 1, chips
    )
    near = ffn(
        own_parts[0], sib_parts[0], x_all, dout_all, wo_own, wo_sib, w_gu, w_down, gain_ffn, 0, chips
    )
    nm_near, gnm_near, lay_near, inner_near, ggu_near, gnf_near, middle, mixed_own = near
    nm_far, gnm_far, lay_far, inner_far, ggu_far, gnf_far = far

    gnm_parts = scatter_plane(gnm_near, gnm_far, seq_count)
    grad_middle, grad_branch, gm_own, gm_sib = middle_back(
        gnm_parts, middle, dout_own, gain_ffn, wo_own, wo_sib
    )
    gm_got = swap(gm_sib, seq_count, 1)
    gm_pairs = jnp.stack([gm_own, gm_got], axis=1)
    gm_here = [gm_pairs[0]] + [swap(gm_pairs[r], seq_count, 2 * r) for r in range(1, chips)]
    g_all = jnp.concatenate([p[0] for p in gm_here] + [p[1] for p in gm_here], axis=0)

    grad_gu = (dot_tn(nm_near, ggu_near) + dot_tn(nm_far, ggu_far)).astype(BF16)
    grad_gu = grad_gu.reshape(seq_count, z_count, shard, 2 * hidden).transpose(1, 0, 2, 3)
    grad_gu = lax.psum_scatter(
        grad_gu.reshape(width, 2 * hidden), "fsdp", scatter_dimension=0, tiled=True
    ).reshape(seq_count, shard, 2 * hidden)
    grad_gu = lax.all_to_all(grad_gu, "seq", split_axis=0, concat_axis=0, tiled=True)
    grad_gu = grad_gu.transpose(1, 0, 2).astype(F32)
    grad_gate = grad_gu[:, :, :hidden].reshape(shard, seq_count * hidden)
    grad_up = grad_gu[:, :, hidden:].reshape(shard, seq_count * hidden)

    dout_near, dout_far = dout_all[:half_rows], dout_all[half_rows:]
    grad_down = (dot_tn(inner_near, dout_near) + dot_tn(inner_far, dout_far)).astype(BF16)
    grad_out = dot_tn(mixed_own, grad_branch).astype(BF16)
    grad_out = add_up(
        scatter_plane(grad_out[: chips * WIDE], grad_out[chips * WIDE :], seq_count)
    ).astype(BF16)[:features]
    down_out = jnp.concatenate(
        [
            grad_down.reshape(z_count, hidden // z_count, width),
            grad_out.reshape(z_count, features // z_count, width),
        ],
        axis=1,
    )
    down_out = lax.psum_scatter(down_out, "fsdp", scatter_dimension=0, tiled=False).astype(F32)
    grad_down = down_out[: hidden // z_count]
    grad_out = down_out[hidden // z_count :]
    layer_out = (middle + add_up(scatter_plane(lay_near, lay_far, seq_count))).astype(BF16)

    dq, dk, dv, bias_rows = attend_back(
        q_aug, g_all, o_all, zi_all, lane_rows, k_aug, k_trans, v_aug, head_size
    )
    back = [
        qkv_back(dq, dk, dv, q_lin, k_lin, lane_rows, w_qkv, x_all, q_gain, k_gain, head_size, half)
        for half in (0, 1)
    ]
    gni_parts = scatter_plane(back[0][0], back[1][0], seq_count)
    in_grad = input_back(gni_parts, x_own, grad_middle, gain_attn)
    grad_qkv = (
        dot_tn(normed_in[:half_rows], back[0][1]) + dot_tn(normed_in[half_rows:], back[1][1])
    ).astype(BF16)
    grad_qkv = lax.all_to_all(
        grad_qkv.reshape(seq_count * z_count, shard, 3 * WIDE),
        ("seq", "fsdp"), split_axis=0, concat_axis=0, tiled=True,
    ).reshape(seq_count, z_count, shard, 3 * WIDE)
    grad_qkv = jnp.sum(grad_qkv.astype(F32), axis=1).transpose(1, 0, 2)
    grad_query, grad_key, grad_value = (
        grad_qkv[:, :, i * WIDE : i * WIDE + features].reshape(shard, width) for i in range(3)
    )

    gain_rows = back[0][2] + back[1][2]
    grad_qk_gain = gain_rows[:2, :features].reshape(2, heads, head_size).sum(axis=1)
    bias_cols = jnp.sum(bias_rows, axis=1).reshape(2, 2, 4).sum(axis=2)[:, :heads]
    bias_both = jnp.stack([bias_cols[0], bias_cols[1] - bias_cols[0]])
    spread = lax.dynamic_update_slice(
        jnp.zeros((2, heads * seq_count), F32), bias_both, (0, me * heads)
    )
    small = jnp.concatenate(
        [
            (back[0][3] + back[1][3]).reshape(-1),
            (gnf_near + gnf_far).reshape(-1),
            grad_qk_gain.reshape(-1),
            spread.reshape(-1),
        ]
    )
    small = lax.psum(small, ("seq", "fsdp"))
    cut = 2 * width + 2 * head_size
    grad_bias = lax.dynamic_slice(
        small[cut:].reshape(2, heads * seq_count), (0, me * heads), (2, heads)
    )
    return (
        layer_out.reshape(tokens.shape),
        in_grad.reshape(tokens.shape),
        grad_query,
        grad_key,
        grad_value,
        grad_out,
        grad_gate,
        grad_up,
        grad_down,
        small[:width],
        small[width : 2 * width],
        small[2 * width : 2 * width + head_size],
        small[2 * width + head_size : cut],
        grad_bias,
    )


def solution(mesh):
    rows = P("fsdp", "seq", None)
    shards = P(("seq", "fsdp"), None)
    ids = P("fsdp", "seq")
    bias = P(None, "seq")
    return jax.shard_map(
        body,
        mesh=mesh,
        in_specs=(rows,) + (shards,) * 7 + (P(),) * 4 + (bias, ids, ids, ids, rows),
        out_specs=(rows, rows) + (shards,) * 7 + (P(),) * 4 + (bias,),
        check_vma=False,
    )
```

time: 2240 us -> 472 us (0.21)
  waiting for transfers between devices: 1760 us -> 74.9 us
  matrix products: 196 us -> 20.7 us
  Pallas kernels: 0 us -> 120 us
  other arithmetic: 69.6 us -> 32.4 us
  starting transfers between devices: 23.6 us -> 58.4 us
    reduce_scatter x7 -> x2, waiting for transfers between devices: 1420 us -> 0.01 us  [the longest x1 0.01 us: body(): lax.psum_scatter(grad_gu.reshape(width, 2 * hidden), 'fsdp', scatter_dime...]
    all_gather x7 -> x2, waiting for transfers between devices: 318 us -> 0.01 us  [the longest x1 0.01 us: body(): lax.all_gather(jnp.concatenate([weight_down, weight_out], axis=0), 'fsdp'...]
    dot_general x49 -> x7, matrix products: 196 us -> 20.7 us  [dot_tn(): lax.dot_general(left, right, (((0,), (0,)), ((), ())), preferred_element_...]
    pallas_call x0 -> x10, Pallas kernels: none -> 120 us  [the longest x2 34 us: ffn(): pl.pallas_call(functools.partial(ffn_kernel, chips=chips, own=own), grid=...]
    ppermute x0 -> x40, waiting for transfers between devices: none -> 74.8 us  [swap(): return lax.ppermute(x, 'seq', [(i, i ^ bits) for i in range(seq_count)])]
    reduce_sum x11 -> x4, other arithmetic: 44.2 us -> 1.51 us  [the longest x1 1.28 us: body(): grad_qkv = jnp.sum(grad_qkv.astype(F32), axis=1).transpose(1, 0, 2)]
    ppermute x0 -> x40, starting transfers between devices: none -> 39.3 us  [swap(): return lax.ppermute(x, 'seq', [(i, i ^ bits) for i in range(seq_count)])]
    all_to_all x2 -> x0, blocking collectives: 32 us -> none  [the longest x1 18.6 us: body(): lax.all_to_all(mixed_heads[:, :, None], 'seq', split_axis=1, concat_axis=...]
  transfers between devices with their start and end apart: 20 -> 48, of which waited for: 16 -> 14; matrix products, arithmetic and copies ran while one was open for 13% -> 21% of each run, Pallas kernels for 0% -> 26%
where the time goes in v1:
time: 472 us; the launch traced here: 466 us
  Pallas kernels  120 us (25%)
  blocking collectives  91.8 us (19%)
  waiting for transfers between devices  74.9 us (16%)
  starting transfers between devices  58.4 us (12%)
  local copies, waits for them, and re-layouts  52.9 us (11%)
  other arithmetic  32.4 us (7%)
  matrix products  20.7 us (4%)
  between operations  14.8 us (3%)
    ppermute x40, waiting for transfers between devices, swap(): return lax.ppermute(x, 'seq', [(i, i ^ bits) for i in range(seq_count)])  74.8 us
    psum x1, blocking collectives, body(): small = lax.psum(small, ('seq', 'fsdp'))  47.7 us
    all_gather x1, blocking collectives, body(): lax.all_gather(jnp.concatenate([variate_ids, sample_ids, time_ids], axis=...  44 us
    ppermute x40, starting transfers between devices, swap(): return lax.ppermute(x, 'seq', [(i, i ^ bits) for i in range(seq_count)])  39.3 us
    pallas_call x2, Pallas kernels, ffn(): pl.pallas_call(functools.partial(ffn_kernel, chips=chips, own=own), grid=...  34 us
    pallas_call x1, Pallas kernels, attend_back(): pl.pallas_call(functools.partial(attend_back_kernel, heads=heads, head_si...  30.4 us
    unnamed x138, local copies, waits for them, and re-layouts  21 us
    dot_general x7, matrix products, dot_tn(): lax.dot_general(left, right, (((0,), (0,)), ((), ())), preferred_element_...  20.7 us
  transfers between devices with their start and end apart: 48, of which 14 were waited for; matrix products, arithmetic and copies ran while one was open for 21% of the time, Pallas kernels for 26%

profile of v1, /device:TPU:0, one launch (start us, length us, event | category | flops | bytes accessed | tf_op | source)
XLA Modules:
  0.0 466.2 jit_solution(16508160912548664753)
XLA Ops:
  7.2 4.0 collective-permute-start.2
  23.0 44.0 %all-gather.3 = s32[8,3,256]{2,1,0:T(4,128)S(1)} all-gather(s32[1,3,256]{2,1,0:T(4,128)S(1)} %add_bitcast_fusion), channel_id=2, replica_groups=mesh['seq'=8,'fsdp'=4] {'seq'}, dimensions={0}, use_global_device_ids=true | all-gather | bytes 27648 | tf_op jit(solution)/shard_map/all_gather | solution.py:605
  75.8 5.4 %all-to-all-start = ((bf16[32,32,384]{2,1,0:T(8,128)(2,1)}), bf16[32,32,384]{2,1,0:T(8,128)(2,1)S(1)}, u32[]{:S(2)}, u32[]{:S(2)}) async-start(bf16[32,32,384]{2,1,0:T(8,128)(2,1)} %bitcast.2), calls=%async_computation | async-start | bytes 1572864 | tf_op jit(solution)/shard_map/all_to_all | solution.py:583
  104.8 5.4 %collective-permute-done.16 = bf16[128,1024]{1,0:T(8,128)(2,1)S(1)} collective-permute-done((bf16[128,1024]{1,0:T(8,128)(2,1)S(1)}, bf16[128,1024]{1,0:T(8,128)(2,1)S(1)}, u32[]{:S(2)}, u32[]{:S(2)}) %collective-permute-start.16) | collective-permute-done | bytes 262176 | tf_op jit(solution)/shard_map/ppermute | solution.py:524
  115.4 11.8 %project.1 = (bf16[2048,1024]{1,0:T(8,128)(2,1)}, f32[2048,128]{1,0:T(8,128)}, f32[2048,128]{1,0:T(8,128)}, bf16[2048,256]{1,0:T(8,128)(2,1)}, bf16[2,2048,256]{...) custom-call(bf16[2048,1024]{1,0:T(8,128)(2,1)} %constant_dynamic-update-slice_fusion.x_ref.refs_8_, ...), custom_call_target="tpu_custom_call" | custom-call | flops 1610612736 | bytes 16777216 | tf_op jit(solution)/shard_map/project/pallas_call | solution.py:139
  127.2 9.6 %attend.2 = (bf16[1024,128]{1,0:T(8,128)(2,1)}, f32[1024,128]{1,0:T(8,128)}, f32[1024,128]{1,0:T(8,128)}) custom-call(bf16[2048,256]{1,0:T(8,128)(2,1)} %get-tuple-element.57.qa_ref, bf16[2,2048,256]{2,1,0:T(8,128)(2,1)} %get-tuple-element.58.ka_ref, bf16[2,2048,256]{2,1,0:T(8,128)(2,1)} %get-tuple-element.59.v1_ref), custom_call_target="tpu_custom_call" | custom-call | flops 4294967296 | bytes 4194304 | tf_op jit(solution)/shard_map/attend/pallas_call | solution.py:194
  140.3 9.6 %attend.3 = (bf16[1024,128]{1,0:T(8,128)(2,1)}, f32[1024,128]{1,0:T(8,128)}, f32[1024,128]{1,0:T(8,128)}) custom-call(bf16[2048,256]{1,0:T(8,128)(2,1)} %get-tuple-element.57.qa_ref, bf16[2,2048,256]{2,1,0:T(8,128)(2,1)} %get-tuple-element.58.ka_ref, bf16[2,2048,256]{2,1,0:T(8,128)(2,1)} %get-tuple-element.59.v1_ref), custom_call_target="tpu_custom_call" | custom-call | flops 4294967296 | bytes 4194304 | tf_op jit(solution)/shard_map/attend/pallas_call | solution.py:194
  159.4 5.2 %collective-permute-done.8.refs_2_ = bf16[1024,128]{1,0:T(8,128)(2,1)S(1)} collective-permute-done((bf16[1024,128]{1,0:T(8,128)(2,1)}, bf16[1024,128]{1,0:T(8,128)(2,1)S(1)}, u32[]{:S(2)}, u32[]{:S(2)}) %collective-permute-start.8) | collective-permute-done | bytes 262176 | tf_op jit(solution)/shard_map/ppermute | solution.py:524
  171.2 16.6 %ffn_half.3 = (bf16[1024,1024]{1,0:T(8,128)(2,1)}, bf16[1024,1024]{1,0:T(8,128)(2,1)}, bf16[1024,1024]{1,0:T(8,128)(2,1)}, bf16[1024,512]{1,0:T(8,128)(2,1)}, bf...) custom-call(bf16[1024,128]{1,0:T(8,128)(2,1)} %get-tuple-element.61.refs_0_, bf16[1024,128]{1,0:T(8,128)(2,1)} %copy-done.36, ...), custom_call_target="tpu_custom_call" | custom-call | flops 8589934592 | bytes 12582912 | tf_op jit(solution)/shard_map/ffn_half/pallas_call | solution.py:370
  190.6 17.4 %ffn_half.2 = (bf16[1024,1024]{1,0:T(8,128)(2,1)}, bf16[1024,1024]{1,0:T(8,128)(2,1)}, bf16[1024,1024]{1,0:T(8,128)(2,1)}, bf16[1024,512]{1,0:T(8,128)(2,1)}, bf...) custom-call(bf16[1024,128]{1,0:T(8,128)(2,1)} %get-tuple-element.60.refs_0_, ...), custom_call_target="tpu_custom_call" | custom-call | flops 8589934592 | bytes 12582912 | tf_op jit(solution)/shard_map/ffn_half/pallas_call | solution.py:370
  208.0 4.8 %fusion.26 = f32[1024,1024]{1,0:T(8,128)S(1)} fusion(bf16[1024,1024]{1,0:T(8,128)(2,1)} %get-tuple-element.91, bf16[1024,1024]{1,0:T(8,128)(2,1)} %get-tuple-element.92), kind=kOutput, calls=%fused_computation.94 | convolution fusion | flops 2147483648 | bytes 8388608 | tf_op jit(solution)/shard_map/dot_general | solution.py:29
  237.3 6.2 %collective-permute-done.27.refs_3_ = bf16[256,1024]{1,0:T(8,128)(2,1)S(1)} collective-permute-done((bf16[256,1024]{1,0:T(8,128)(2,1)S(1)}, bf16[256,1024]{1,0:T(8,128)(2,1)S(1)}, u32[]{:S(2)}, u32[]{:S(2)}) %collective-permute-start.27) | collective-permute-done | bytes 524320 | tf_op jit(solution)/shard_map/ppermute | solution.py:524
  244.3 10.0 %collective-permute-done.26.refs_2_ = bf16[256,1024]{1,0:T(8,128)(2,1)S(1)} collective-permute-done((bf16[256,1024]{1,0:T(8,128)(2,1)S(1)}, bf16[256,1024]{1,0:T(8,128)(2,1)S(1)}, u32[]{:S(2)}, u32[]{:S(2)}) %collective-permute-start.26) | collective-permute-done | bytes 524320 | tf_op jit(solution)/shard_map/ppermute | solution.py:524
  255.3 5.3 %middle_back.1 = (f32[256,1024]{1,0:T(8,128)}, bf16[256,1024]{1,0:T(8,128)(2,1)}, bf16[4,256,128]{2,1,0:T(8,128)(2,1)}, bf16[4,256,128]{2,1,0:T(8,128)(2,1)}) custom-call(bf16[256,1024]{1,0:T(8,128)(2,1)} %get-tuple-element.107.refs_0_, bf16[256,1024]{1,0:T(8,128)(2,1)} %copy-done.19, bf16[256,1024]{1,0:T(8,128)(2,1)} %copy-done.18, ...), custom_call_target="tpu_custom_call" | custom-call | flops 536870912 | bytes 3145728 | tf_op jit(solution)/shard_map/middle_back/pallas_call | solution.py:414
  266.4 12.7 %collective-permute-done.29 = bf16[2,256,128]{2,1,0:T(8,128)(2,1)S(1)} collective-permute-done((bf16[2,256,128]{2,1,0:T(8,128)(2,1)S(1)}, bf16[2,256,128]{2,1,0:T(8,128)(2,1)S(1)}, u32[]{:S(2)}, u32[]{:S(2)}) %collective-permute-start.29) | collective-permute-done | bytes 131104 | tf_op jit(solution)/shard_map/ppermute | solution.py:524
  280.1 4.1 collective-permute-done.30
  286.2 3.9 collective-permute-done.31
  291.4 30.4 %attend_back.1 = (bf16[2048,128]{1,0:T(8,128)(2,1)}, bf16[2048,128]{1,0:T(8,128)(2,1)}, bf16[2048,128]{1,0:T(8,128)(2,1)}, f32[16,256]{1,0:T(8,128)}) custom-call(bf16[2048,256]{1,0:T(8,128)(2,1)} %get-tuple-element.57.qa_ref, bf16[2048,128]{1,0:T(8,128)(2,1)} %copy-done.40, f32[2048,128]{1,0:T(8,128)} %pad_maximum_fusion.6.o_ref, ...), custom_call_target="tpu_custom_call" | custom-call | flops 17179869184 | bytes 8388608 | tf_op jit(solution)/shard_map/attend_back/pallas_call | solution.py:276
  321.8 8.0 %qkv_back.3 = (bf16[1024,1024]{1,0:T(8,128)(2,1)}, bf16[1024,384]{1,0:T(8,128)(2,1)}, f32[8,128]{1,0:T(8,128)}, f32[1,1024]{1,0:T(1,128)}) custom-call(bf16[2048,128]{1,0:T(8,128)(2,1)} %get-tuple-element.74.dq_ref, bf16[2048,128]{1,0:T(8,128)(2,1)} %get-tuple-element.75.dk_ref, bf16[2048,128]{1,0:T(8,128)(2,1)} %get-tuple-element.76.dv_ref, ...), custom_call_target="tpu_custom_call" | custom-call | flops 805306368 | bytes 6291456 | tf_op jit(solution)/shard_map/qkv_back/pallas_call | solution.py:497
  329.8 8.0 %qkv_back.2 = (bf16[1024,1024]{1,0:T(8,128)(2,1)}, bf16[1024,384]{1,0:T(8,128)(2,1)}, f32[8,128]{1,0:T(8,128)}, f32[1,1024]{1,0:T(1,128)}) custom-call(bf16[2048,128]{1,0:T(8,128)(2,1)} %get-tuple-element.74.dq_ref, bf16[2048,128]{1,0:T(8,128)(2,1)} %get-tuple-element.75.dk_ref, bf16[2048,128]{1,0:T(8,128)(2,1)} %get-tuple-element.76.dv_ref, ...), custom_call_target="tpu_custom_call" | custom-call | flops 805306368 | bytes 6291456 | tf_op jit(solution)/shard_map/qkv_back/pallas_call | solution.py:497
  351.3 6.3 %all-to-all-start.2 = ((bf16[32,32,384]{2,1,0:T(8,128)(2,1)}), bf16[32,32,384]{2,1,0:T(8,128)(2,1)}, u32[]{:S(2)}, u32[]{:S(2)}) async-start(bf16[32,32,384]{2,1,0:T(8,128)(2,1)} %bitcast.167), calls=%async_computation.2 | async-start | bytes 1572864 | tf_op jit(solution)/shard_map/all_to_all | solution.py:699
  365.1 47.7 %psum.7 = f32[2208]{0:T(1024)S(1)} all-reduce(f32[2208]{0:T(1024)S(1)} %pad_maximum_fusion.10), channel_id=1, replica_groups=mesh['seq'=8,'fsdp'=4] {'seq','fsdp'}, use_global_device_ids=true, to_apply=%region_6.7 | all-reduce | flops 2208 | bytes 17664 | tf_op jit(solution)/shard_map/psum | solution.py:723
  431.1 10.4 %collective-permute-done.35.refs_3_ = bf16[256,1024]{1,0:T(8,128)(2,1)S(1)} collective-permute-done((bf16[256,1024]{1,0:T(8,128)(2,1)}, bf16[256,1024]{1,0:T(8,128)(2,1)S(1)}, u32[]{:S(2)}, u32[]{:S(2)}) %collective-permute-start.35) | collective-permute-done | bytes 524320 | tf_op jit(solution)/shard_map/ppermute | solution.py:524
  441.5 10.8 %collective-permute-done.34.refs_2_ = bf16[256,1024]{1,0:T(8,128)(2,1)S(1)} collective-permute-done((bf16[256,1024]{1,0:T(8,128)(2,1)S(1)}, bf16[256,1024]{1,0:T(8,128)(2,1)S(1)}, u32[]{:S(2)}, u32[]{:S(2)}) %collective-permute-start.34) | collective-permute-done | bytes 524320 | tf_op jit(solution)/shard_map/ppermute | solution.py:524
  (316 shorter events, 153.8 us)
Async XLA Ops:
  7.2 63.3 %collective-permute-start.2 = (bf16[256,1024]{1,0:T(8,128)(2,1)}, bf16[256,1024]{1,0:T(8,128)(2,1)S(1)}, u32[]{:S(2)}, u32[]{:S(2)}) collective-permute-start(bf16[256,1024]{1,0:T(8,128)(2,1)} %bitcast.144), channel_id=1, source_target_pairs={{0,24},{4,28},{8,16},{12,20},{16,8},{20,12},{24,0},{28,4},{1,25},{... | collective-permute-start | bytes 1572872 | tf_op jit(solution)/shard_map/ppermute | solution.py:524
  11.1 59.8 %collective-permute-start.1 = (bf16[256,1024]{1,0:T(8,128)(2,1)}, bf16[256,1024]{1,0:T(8,128)(2,1)}, u32[]{:S(2)}, u32[]{:S(2)}) collective-permute-start(bf16[256,1024]{1,0:T(8,128)(2,1)} %bitcast.145), channel_id=1, source_target_pairs={{0,16},{4,20},{8,24},{12,28},{16,0},{20,4},{24,8},{28,12},{1,17},{... | collective-permute-start | bytes 1572872 | tf_op jit(solution)/shard_map/ppermute | solution.py:524
  11.6 59.3 %collective-permute-start = (bf16[256,1024]{1,0:T(8,128)(2,1)}, bf16[256,1024]{1,0:T(8,128)(2,1)}, u32[]{:S(2)}, u32[]{:S(2)}) collective-permute-start(bf16[256,1024]{1,0:T(8,128)(2,1)} %bitcast.146), channel_id=1, source_target_pairs={{0,8},{4,12},{8,0},{12,4},{16,24},{20,28},{24,16},{28,20},{1,9},{5... | collective-permute-start | bytes 1572872 | tf_op jit(solution)/shard_map/ppermute | solution.py:524
  11.8 72.4 %collective-permute-start.13 = (bf16[256,1024]{1,0:T(8,128)(2,1)}, bf16[256,1024]{1,0:T(8,128)(2,1)S(1)}, u32[]{:S(2)}, u32[]{:S(2)}) collective-permute-start(bf16[256,1024]{1,0:T(8,128)(2,1)} %bitcast.138), channel_id=1, source_target_pairs={{0,24},{4,28},{8,16},{12,20},{16,8},{20,12},{24,0},{28,4},{1,25},{... | collective-permute-start | bytes 1572872 | tf_op jit(solution)/shard_map/ppermute | solution.py:524
  14.6 69.6 %collective-permute-start.12 = (bf16[256,1024]{1,0:T(8,128)(2,1)}, bf16[256,1024]{1,0:T(8,128)(2,1)S(1)}, u32[]{:S(2)}, u32[]{:S(2)}) collective-permute-start(bf16[256,1024]{1,0:T(8,128)(2,1)} %bitcast.139), channel_id=1, source_target_pairs={{0,16},{4,20},{8,24},{12,28},{16,0},{20,4},{24,8},{28,12},{1,17},{... | collective-permute-start | bytes 1572872 | tf_op jit(solution)/shard_map/ppermute | solution.py:524
  18.5 56.2 %all-to-all-start.1 = ((bf16[8,32,1024]{2,1,0:T(8,128)(2,1)}), bf16[8,32,1024]{2,1,0:T(8,128)(2,1)S(1)}, u32[]{:S(2)}, u32[]{:S(2)}) async-start(bf16[8,32,1024]{2,1,0:T(8,128)(2,1)} %copy.57), calls=%async_computation.1 | async-start | bytes 1048576 | tf_op jit(solution)/shard_map/all_to_all | solution.py:598
  22.0 71.0 %all-gather.7.cloned.1.call-start = ((), (), s32[]{:S(2)}) async-start(), calls=%async_computation.8 | async-start | bytes 1638400 | tf_op jit(solution)/shard_map/all_gather | solution.py:588
  73.6 37.7 %collective-permute-start.3 = (bf16[1024,1024]{1,0:T(8,128)(2,1)}, bf16[1024,1024]{1,0:T(8,128)(2,1)}, u32[]{:S(2)}, u32[]{:S(2)}) collective-permute-start(bf16[1024,1024]{1,0:T(8,128)(2,1)} %pad_maximum_fusion), channel_id=1, source_target_pairs={{0,4},{4,0},{8,12},{12,8},{16,20},{20,16},{24,28},{28,24},{1,5},{5... | collective-permute-start | bytes 6291464 | tf_op jit(solution)/shard_map/ppermute | solution.py:524
  75.8 38.7 %all-to-all-start = ((bf16[32,32,384]{2,1,0:T(8,128)(2,1)}), bf16[32,32,384]{2,1,0:T(8,128)(2,1)S(1)}, u32[]{:S(2)}, u32[]{:S(2)}) async-start(bf16[32,32,384]{2,1,0:T(8,128)(2,1)} %bitcast.2), calls=%async_computation | async-start | bytes 1572864 | tf_op jit(solution)/shard_map/all_to_all | solution.py:583
  81.2 84.6 %all-gather.9.cloned.1.call-start = ((), (), s32[]{:S(2)}) async-start(), calls=%async_computation.9 | async-start | bytes 2621440 | tf_op jit(solution)/shard_map/all_gather | solution.py:600
  84.1 330.6 %reduce-scatter.5.cloned.1.call-start = ((), (), s32[]{:S(2)}) async-start(), calls=%async_computation.7 | async-start | bytes 2621440 | tf_op jit(solution)/shard_map/reduce_scatter | solution.py:661
  88.3 67.3 %collective-permute-start.14 = (bf16[1024,1024]{1,0:T(8,128)(2,1)}, bf16[1024,1024]{1,0:T(8,128)(2,1)S(1)}, u32[]{:S(2)}, u32[]{:S(2)}) collective-permute-start(bf16[1024,1024]{1,0:T(8,128)(2,1)} %pad_maximum_fusion.1), channel_id=1, source_target_pairs={{0,4},{4,0},{8,12},{12,8},{16,20},{20,16},{24,28},{28,24},{1,5},{5... | collective-permute-start | bytes 6291464 | tf_op jit(solution)/shard_map/ppermute | solution.py:524
  111.3 59.9 %collective-permute-start.18 = (bf16[512,1024]{1,0:T(8,128)(2,1)}, bf16[512,1024]{1,0:T(8,128)(2,1)}, u32[]{:S(2)}, u32[]{:S(2)}) collective-permute-start(bf16[512,1024]{1,0:T(8,128)(2,1)} %pad_maximum_fusion.4.refs_10_.refs_7_), channel_id=1, source_target_pairs={{0,4},{4,0},{8,12},{12,8},{16,20},{20,16},{24,28},{28,24},{1,5},{5... | collective-permute-start | bytes 3145736 | tf_op jit(solution)/shard_map/ppermute | solution.py:524
  187.8 43.5 %collective-permute-start.20 = (bf16[1024,1024]{1,0:T(8,128)(2,1)}, bf16[1024,1024]{1,0:T(8,128)(2,1)}, u32[]{:S(2)}, u32[]{:S(2)}) collective-permute-start(bf16[1024,1024]{1,0:T(8,128)(2,1)} %get-tuple-element.64), channel_id=1, source_target_pairs={{0,4},{4,0},{8,12},{12,8},{16,20},{20,16},{24,28},{28,24},{1,5},{5... | collective-permute-start | bytes 6291464 | tf_op jit(solution)/shard_map/ppermute | solution.py:524
  188.4 35.6 %collective-permute-start.24 = (bf16[1024,1024]{1,0:T(8,128)(2,1)}, bf16[1024,1024]{1,0:T(8,128)(2,1)}, u32[]{:S(2)}, u32[]{:S(2)}) collective-permute-start(bf16[1024,1024]{1,0:T(8,128)(2,1)} %get-tuple-element.66), channel_id=1, source_target_pairs={{0,4},{4,0},{8,12},{12,8},{16,20},{20,16},{24,28},{28,24},{1,5},{5... | collective-permute-start | bytes 6291464 | tf_op jit(solution)/shard_map/ppermute | solution.py:524
  229.4 24.9 %collective-permute-start.26 = (bf16[256,1024]{1,0:T(8,128)(2,1)S(1)}, bf16[256,1024]{1,0:T(8,128)(2,1)S(1)}, u32[]{:S(2)}, u32[]{:S(2)}) collective-permute-start(bf16[256,1024]{1,0:T(8,128)(2,1)S(1)} %get-tuple-element.105), channel_id=1, source_target_pairs={{0,16},{4,20},{8,24},{12,28},{16,0},{20,4},{24,8},{28,12},{1,17},{... | collective-permute-start | bytes 1572872 | tf_op jit(solution)/shard_map/ppermute | solution.py:524
  235.1 126.6 %collective-permute-start.21 = (bf16[256,1024]{1,0:T(8,128)(2,1)}, bf16[256,1024]{1,0:T(8,128)(2,1)}, u32[]{:S(2)}, u32[]{:S(2)}) collective-permute-start(bf16[256,1024]{1,0:T(8,128)(2,1)} %get-tuple-element.108), channel_id=1, source_target_pairs={{0,8},{4,12},{8,0},{12,4},{16,24},{20,28},{24,16},{28,20},{1,9},{5... | collective-permute-start | bytes 1572872 | tf_op jit(solution)/shard_map/ppermute | solution.py:524
  236.9 124.9 %collective-permute-start.23 = (bf16[256,1024]{1,0:T(8,128)(2,1)}, bf16[256,1024]{1,0:T(8,128)(2,1)}, u32[]{:S(2)}, u32[]{:S(2)}) collective-permute-start(bf16[256,1024]{1,0:T(8,128)(2,1)} %get-tuple-element.109), channel_id=1, source_target_pairs={{0,24},{4,28},{8,16},{12,20},{16,8},{20,12},{24,0},{28,4},{1,25},{... | collective-permute-start | bytes 1572872 | tf_op jit(solution)/shard_map/ppermute | solution.py:524
  243.5 118.2 %collective-permute-start.22 = (bf16[256,1024]{1,0:T(8,128)(2,1)}, bf16[256,1024]{1,0:T(8,128)(2,1)}, u32[]{:S(2)}, u32[]{:S(2)}) collective-permute-start(bf16[256,1024]{1,0:T(8,128)(2,1)} %get-tuple-element.110), channel_id=1, source_target_pairs={{0,16},{4,20},{8,24},{12,28},{16,0},{20,4},{24,8},{28,12},{1,17},{... | collective-permute-start | bytes 1572872 | tf_op jit(solution)/shard_map/ppermute | solution.py:524
  264.1 73.8 %collective-permute-start.36 = (bf16[512,1024]{1,0:T(8,128)(2,1)S(1)}, bf16[512,1024]{1,0:T(8,128)(2,1)}, u32[]{:S(2)}, u32[]{:S(2)}) collective-permute-start(bf16[512,1024]{1,0:T(8,128)(2,1)S(1)} %slice.300), channel_id=1, source_target_pairs={{0,4},{4,0},{8,12},{12,8},{16,20},{20,16},{24,28},{28,24},{1,5},{5... | collective-permute-start | bytes 3145736 | tf_op jit(solution)/shard_map/ppermute | solution.py:524
  351.3 63.5 %all-to-all-start.2 = ((bf16[32,32,384]{2,1,0:T(8,128)(2,1)}), bf16[32,32,384]{2,1,0:T(8,128)(2,1)}, u32[]{:S(2)}, u32[]{:S(2)}) async-start(bf16[32,32,384]{2,1,0:T(8,128)(2,1)} %bitcast.167), calls=%async_computation.2 | async-start | bytes 1572864 | tf_op jit(solution)/shard_map/all_to_all | solution.py:699
  357.6 99.4 %reduce-scatter.3.cloned.1.call-start = ((), (), s32[]{:S(2)}) async-start(), calls=%async_computation.6 | async-start | bytes 1638400 | tf_op jit(solution)/shard_map/reduce_scatter | solution.py:682
  357.7 64.2 %collective-permute-start.32 = (bf16[1024,1024]{1,0:T(8,128)(2,1)}, bf16[1024,1024]{1,0:T(8,128)(2,1)}, u32[]{:S(2)}, u32[]{:S(2)}) collective-permute-start(bf16[1024,1024]{1,0:T(8,128)(2,1)} %get-tuple-element.80), channel_id=1, source_target_pairs={{0,4},{4,0},{8,12},{12,8},{16,20},{20,16},{24,28},{28,24},{1,5},{5... | collective-permute-start | bytes 6291464 | tf_op jit(solution)/shard_map/ppermute | solution.py:524
  428.6 23.8 %collective-permute-start.34 = (bf16[256,1024]{1,0:T(8,128)(2,1)S(1)}, bf16[256,1024]{1,0:T(8,128)(2,1)S(1)}, u32[]{:S(2)}, u32[]{:S(2)}) collective-permute-start(bf16[256,1024]{1,0:T(8,128)(2,1)S(1)} %get-tuple-element.101), channel_id=1, source_target_pairs={{0,16},{4,20},{8,24},{12,28},{16,0},{20,4},{24,8},{28,12},{1,17},{... | collective-permute-start | bytes 1572872 | tf_op jit(solution)/shard_map/ppermute | solution.py:524
  (82 other events, 767.4 us)
Sparse Core Ops, SparseCore 0:
  25.0 34.3 all-gather.6
  84.3 51.6 all-gather.8
  217.1 45.4 reduce-scatter.4
  361.8 38.1 reduce-scatter.2

commit v2 on v1

v2 whole, which is shorter than its diff:
```python
import functools
import math

import jax
import jax.numpy as jnp
from jax import lax
from jax.experimental import pallas as pl
from jax.experimental.pallas import tpu as pltpu
from jax.sharding import PartitionSpec as P

EPSILON = 1e-06
FAR = -1e30
LOG2E = math.log2(math.e)
WIDE = 128
ROWS_T = 160
F32 = jnp.float32
BF16 = jnp.bfloat16


def dot_nn(left, right):
    return jnp.dot(left, right, preferred_element_type=F32)


def dot_nt(left, right):
    return lax.dot_general(left, right, (((1,), (1,)), ((), ())), preferred_element_type=F32)


def dot_tn(left, right):
    return lax.dot_general(left, right, (((0,), (0,)), ((), ())), preferred_element_type=F32)


def rms_factor(values):
    return lax.rsqrt(jnp.mean(values * values, axis=-1, keepdims=True) + EPSILON)


def lanes_of(shape):
    return lax.broadcasted_iota(jnp.int32, shape, len(shape) - 1)


def head_sum(values, blocks):
    high = values.astype(BF16)
    low = (values - high.astype(F32)).astype(BF16)
    return dot_nn(high, blocks) + dot_nn(low, blocks)


def head_blocks(head_size):
    row = lax.broadcasted_iota(jnp.int32, (WIDE, WIDE), 0) // head_size
    column = lax.broadcasted_iota(jnp.int32, (WIDE, WIDE), 1) // head_size
    return jnp.where(row == column, 1.0, 0.0).astype(BF16)


def partner(values, lane, head_size):
    half = head_size // 2
    up = pltpu.roll(values, WIDE - half, 1)
    down = pltpu.roll(values, half, 1)
    return jnp.where(lane % head_size < half, up, down)


def tables(cosine, sine):
    times = WIDE // (2 * cosine.shape[0])
    cos_rows = jnp.concatenate([cosine, cosine] * times, axis=0)
    sin_rows = jnp.concatenate([-sine, sine] * times, axis=0)
    return cos_rows.T, sin_rows.T


def params(grid=True):
    return pltpu.CompilerParams(
        vmem_limit_bytes=60 * 1024 * 1024,
        dimension_semantics=("arbitrary",) if grid else None,
    )


def whole(array):
    return pl.BlockSpec(array.shape, lambda *_: (0,) * len(array.shape))


def shaped(shape, dtype):
    return jax.ShapeDtypeStruct(shape, dtype)


ANY = pl.BlockSpec(memory_space=pl.ANY)


def assemble(out_ref, in_ref):
    if len(in_ref.shape) == 2:
        out_ref[...] = in_ref[...]
        return
    z_count, seq_count, shard, _ = in_ref.shape
    for f in range(z_count):
        for s in range(seq_count):
            at = (s * z_count + f) * shard
            out_ref[at : at + shard, :] = in_ref[f, s]


def gathered(w):
    if w.shape[2] % 16 == 0:
        return w
    return w.transpose(1, 0, 2, 3).reshape(-1, w.shape[-1])


def columns_kernel(*refs):
    *weights, out_ref = refs
    at = 0
    for w_ref in weights:
        wide = w_ref.shape[1] // out_ref.shape[0]
        for s in range(out_ref.shape[0]):
            out_ref[s, :, at : at + wide] = w_ref[:, s * wide : (s + 1) * wide]
        at += wide


def columns_by_device(weights, seq_count):
    shard = weights[0].shape[0]
    wides = [w.shape[1] // seq_count for w in weights]
    if shard % 16 == 0 and all(wide % WIDE == 0 for wide in wides):
        return pl.pallas_call(
            columns_kernel,
            out_shape=shaped((seq_count, shard, sum(wides)), BF16),
            compiler_params=params(False),
            name="columns",
        )(*weights)
    pieces = []
    for w, wide in zip(weights, wides):
        short = -wide % WIDE
        pieces.append(jnp.pad(w.reshape(shard, seq_count, wide), ((0, 0), (0, 0), (0, short))))
    return jnp.concatenate(pieces, axis=2).transpose(1, 0, 2)


def project_kernel(
    x_ref, w_ref, na_ref, qg_ref, kg_ref, freq_ref, bias_ref,
    nin_ref, qlin_ref, klin_ref, lane_ref, qa_ref, ka_ref, kt_ref, v1_ref, w_s, *, heads, head_size,
):
    half = head_size // 2
    rows = nin_ref.shape[0]

    @pl.when(pl.program_id(0) == 0)
    def _():
        assemble(w_s, w_ref)

    x = x_ref[:rows, :].astype(F32)
    ids = x_ref[rows:, :rows].astype(F32)
    nin = (x * rms_factor(x) * na_ref[...]).astype(BF16)
    nin_ref[...] = nin
    lin = dot_nn(nin, w_s[...])
    q, k, v = lin[:, :WIDE], lin[:, WIDE : 2 * WIDE], lin[:, 2 * WIDE :]
    qlin_ref[...] = q
    klin_ref[...] = k
    angles = freq_ref[...] * (ids[2:3] * 64.0 + ids[3:4])
    cosine, sine = jnp.cos(angles), jnp.sin(angles)
    lane_ref[...] = jnp.concatenate([cosine, sine, ids[:8]], axis=0)
    cosine, sine = tables(cosine, sine)
    lane = lanes_of((rows, WIDE))
    blocks = head_blocks(head_size)

    def finish(u, gain):
        factor = lax.rsqrt(head_sum(u * u, blocks) * (1.0 / head_size) + EPSILON)
        u = u * factor * gain
        return u * cosine + partner(u, lane, head_size) * sine

    q = finish(q, qg_ref[...]) * (LOG2E * head_size**-0.5)
    k = finish(k, kg_ref[...])
    few = ROWS_T - WIDE
    row = lax.broadcasted_iota(jnp.int32, (few, rows), 0)
    variate = ids[0:1].astype(jnp.int32)
    sample = ids[1:2].astype(jnp.int32)
    same_variate = (row % 4) == variate
    same_sample = (row - 10) == sample
    one = jnp.ones((few, rows), F32)
    nil = jnp.zeros((few, rows), F32)
    rest = jnp.zeros((WIDE - few, rows), F32)

    def columns(few_rows):
        return jnp.concatenate([few_rows, rest], axis=0).T

    aug_q = jnp.where(
        row < 8,
        jnp.where(same_variate, one, nil),
        jnp.where(row < 10, one, jnp.where((row < 13) & same_sample, one, nil)),
    )
    qa_ref[...] = jnp.concatenate([q, columns(aug_q)], axis=1).astype(BF16)
    k_t = k.T
    row_k = lax.broadcasted_iota(jnp.int32, (WIDE, rows), 0)
    for h in range(heads):
        first, second = bias_ref[0, h] * LOG2E, bias_ref[1, h] * LOG2E
        step_up = jnp.where(row < 8, first - second, second) * one
        high = step_up.astype(BF16).astype(F32)
        low = step_up - high
        far = jnp.where(same_sample, nil, FAR)
        plain = jnp.where(((row // 4) == 4 + h) & same_variate, one, nil)
        aug_k = jnp.where(
            row < 4,
            jnp.where(same_variate, high, nil),
            jnp.where(
                row < 8,
                jnp.where(same_variate, low, nil),
                jnp.where(
                    row == 8,
                    high,
                    jnp.where(row == 9, low, jnp.where(row < 13, far, plain)),
                ),
            ),
        )
        mine = (lane // head_size) == h
        mine_t = (row_k // head_size) == h
        ka_ref[h] = jnp.concatenate([jnp.where(mine, k, 0.0), columns(aug_k)], axis=1).astype(BF16)
        kt_ref[h] = jnp.concatenate([jnp.where(mine_t, k_t, 0.0), aug_k], axis=0).astype(BF16)
        ones_v = jnp.where((lane == h) | (lane == 2 + h), 1.0, 0.0)
        v1_ref[h] = jnp.concatenate([jnp.where(mine, v, 0.0), ones_v], axis=1).astype(BF16)


def project(x, chips, w, norm_attn, q_gain, k_gain, freq, bias, head_size):
    width, wide = x.shape[1], w.shape[-1]
    rows = x.shape[0] // chips - 16
    heads = bias.shape[1]
    half = chips * rows
    count = head_size + 8
    row_block = lambda cols: pl.BlockSpec((rows, cols), lambda i: (i, 0))
    lane_block = pl.BlockSpec((count, rows), lambda i: (0, i))
    head_block = pl.BlockSpec((heads, rows, 2 * WIDE), lambda i: (0, i, 0))
    return pl.pallas_call(
        functools.partial(project_kernel, heads=heads, head_size=head_size),
        grid=(chips,),
        in_specs=[pl.BlockSpec((rows + 16, width), lambda i: (i, 0))]
        + [whole(a) for a in (w, norm_attn, q_gain, k_gain, freq)]
        + [pl.BlockSpec(memory_space=pltpu.SMEM)],
        out_specs=[
            row_block(width), row_block(WIDE), row_block(WIDE), lane_block, row_block(2 * WIDE),
            head_block, pl.BlockSpec((heads, ROWS_T, rows), lambda i: (0, 0, i)), head_block,
        ],
        out_shape=[
            shaped((half, width), BF16),
            shaped((half, WIDE), F32),
            shaped((half, WIDE), F32),
            shaped((count, half), F32),
            shaped((half, 2 * WIDE), BF16),
            shaped((heads, half, 2 * WIDE), BF16),
            shaped((heads, ROWS_T, half), BF16),
            shaped((heads, half, 2 * WIDE), BF16),
        ],
        scratch_shapes=[pltpu.VMEM((width, wide), BF16)],
        compiler_params=params(),
        cost_estimate=pl.CostEstimate(
            flops=2 * half * width * 3 * WIDE, bytes_accessed=half * width * 8, transcendentals=0
        ),
        name="project",
    )(x, w, norm_attn, q_gain, k_gain, freq, bias)


def attend_kernel(qa_ref, ka0, ka1, v10, v11, mixed_ref, o_ref, zi_ref, *, heads, head_size, chunk):
    qa = qa_ref[...]
    rows = qa.shape[0]
    half = ka0.shape[1]
    lane = lanes_of((rows, WIDE))
    total = jnp.zeros((rows, WIDE), F32)
    inverse = jnp.ones((rows, WIDE), F32)
    for h in range(heads):
        acc = jnp.zeros((rows, 2 * WIDE), F32)
        for ka_ref, v1_ref in ((ka0, v10), (ka1, v11)):
            for c in range(half // chunk):
                part = pl.ds(c * chunk, chunk)
                e = jnp.exp2(dot_nt(qa, ka_ref[h, part, :])).astype(BF16)
                acc = acc + dot_nn(e, v1_ref[h, part, :])
        z_inv = 1.0 / acc[:, WIDE + h : WIDE + h + 1]
        total = total + acc[:, :WIDE] * z_inv
        inverse = jnp.where((lane // head_size) == h, z_inv, inverse)
    mixed_ref[...] = total.astype(BF16)
    o_ref[...] = total
    zi_ref[...] = inverse


def attend(qa, ka, v1, head_size, block=512, chunk=256):
    heads, half, _ = ka[0].shape
    out_block = pl.BlockSpec((block, WIDE), lambda i: (i, 0))
    return pl.pallas_call(
        functools.partial(attend_kernel, heads=heads, head_size=head_size, chunk=chunk),
        grid=(half // block,),
        in_specs=[pl.BlockSpec((block, 2 * WIDE), lambda i: (i, 0))]
        + [whole(a) for a in (*ka, *v1)],
        out_specs=[out_block, out_block, out_block],
        out_shape=[shaped((half, WIDE), BF16), shaped((half, WIDE), F32), shaped((half, WIDE), F32)],
        compiler_params=params(),
        cost_estimate=pl.CostEstimate(
            flops=2 * heads * half * half * 8 * WIDE,
            bytes_accessed=half * WIDE * 32,
            transcendentals=2 * heads * half * half,
        ),
        name="attend",
    )(qa, *ka, *v1)


def attend_back_kernel(*refs, chips, heads, head_size, chunk):
    me_ref, g_ref = refs[:2]
    at = 2
    qa, o, zi, lanes, ka, kt, v1 = [refs[at + 2 * n : at + 2 * n + 2] for n in range(7)]
    at += 14
    dq_refs = refs[at : at + 2]
    dk_ref, dv_ref, bias_ref, g_s, dk_s, dv_s = refs[at + 2 :]
    step = pl.program_id(0)

    @pl.when(step == 0)
    def _():
        dk_s[...] = jnp.zeros_like(dk_s)
        dv_s[...] = jnp.zeros_like(dv_s)
        bias_ref[...] = jnp.zeros_like(bias_ref)
        for j in range(2 * chips):
            g_s[j % 2, j // 2] = g_ref[me_ref[0] ^ j]

    for side in range(2):
        q_rows = qa[side][...]
        rows = q_rows.shape[0]
        half_len = ka[0].shape[1]
        lane = lanes_of((rows, WIDE))
        q = q_rows[:, :WIDE]
        gz = (g_s[side, step].astype(F32) * zi[side][...]).astype(BF16)
        inner = gz.astype(F32) * o[side][...]
        aug = jnp.zeros((rows, WIDE), F32)
        for h in range(heads):
            mean = -jnp.sum(
                jnp.where((lane // head_size) == h, inner, 0.0), axis=-1, keepdims=True
            ) * jnp.ones((rows, WIDE), F32)
            high = mean.astype(BF16).astype(F32)
            aug = jnp.where(lane == h, high, jnp.where(lane == 2 + h, mean - high, aug))
        ga = jnp.concatenate([gz, aug.astype(BF16)], axis=1)
        dq_t = jnp.zeros((ROWS_T, rows), F32)
        for h in range(heads):
            mine = (lane // head_size) == h
            q_h = jnp.where(mine, q, jnp.zeros_like(q))
            g_h = jnp.where(mine, gz, jnp.zeros_like(gz))
            for other in range(2):
                for c in range(half_len // chunk):
                    part = pl.ds(c * chunk, chunk)
                    e = jnp.exp2(dot_nt(ka[other][h, part, :], q_rows))
                    ds = (e * dot_nt(v1[other][h, part, :], ga)).astype(BF16)
                    dv_s[other, part, :] += dot_nn(e.astype(BF16), g_h)
                    dk_s[other, part, :] += dot_nn(ds, q_h)
                    dq_t = dq_t + dot_nn(kt[other][h, :, part], ds)
        dq_refs[side][...] = (dq_t[:WIDE].T * (head_size**-0.5)).astype(BF16)
        variate = lanes[side][head_size : head_size + 1, :].astype(jnp.int32)
        columns = dq_t[WIDE + 16 : WIDE + 24]
        row = lax.broadcasted_iota(jnp.int32, columns.shape, 0)
        bias_ref[...] += jnp.concatenate(
            [jnp.where((row % 4) == variate, columns, 0.0), columns], axis=0
        )

    @pl.when(step == pl.num_programs(0) - 1)
    def _():
        dk_ref[...] = (dk_s[...] * (1.0 / LOG2E)).astype(BF16)
        dv_ref[...] = dv_s[...].astype(BF16)


def attend_back(me, g, qa, o, zi, lane_rows, ka, kt, v1, head_size, chunk=1024):
    heads, half, _ = ka[0].shape
    chips = g.shape[0] // 2
    chunk = math.gcd(half, chunk)
    block = half // chips
    count = lane_rows[0].shape[0]
    row_block = lambda cols: pl.BlockSpec((block, cols), lambda i: (i, 0))
    lane_block = pl.BlockSpec((count, block), lambda i: (0, i))
    full = shaped((2, half, WIDE), BF16)
    return pl.pallas_call(
        functools.partial(
            attend_back_kernel, chips=chips, heads=heads, head_size=head_size, chunk=chunk
        ),
        grid=(chips,),
        in_specs=[pl.BlockSpec(memory_space=pltpu.SMEM), whole(g)]
        + [row_block(2 * WIDE)] * 2
        + [row_block(WIDE)] * 4
        + [lane_block] * 2
        + [whole(a) for a in (*ka, *kt, *v1)],
        out_specs=[row_block(WIDE)] * 2
        + [whole(full), whole(full), pl.BlockSpec((16, block), lambda i: (0, 0))],
        out_shape=[shaped((half, WIDE), BF16)] * 2 + [full, full, shaped((16, block), F32)],
        scratch_shapes=[
            pltpu.VMEM((2, chips, block, WIDE), BF16),
            pltpu.VMEM((2, half, WIDE), F32),
            pltpu.VMEM((2, half, WIDE), F32),
        ],
        compiler_params=params(),
        cost_estimate=pl.CostEstimate(
            flops=2 * heads * half * half * 32 * WIDE,
            bytes_accessed=half * WIDE * 64,
            transcendentals=4 * heads * half * half,
        ),
        name="attend_back",
    )(me, g, *qa, *o, *zi, *lane_rows, *ka, *kt, *v1)


def ffn_kernel(*refs, chips, near):
    mixed = refs[: 2 * chips]
    extra_parts = refs[2 * chips : 4 * chips]
    at = 4 * chips
    x_ref, wgu_ref, wd_ref, nf_ref = refs[at : at + 4]
    at += 4
    if near:
        got_ref, lay_got_ref = refs[at : at + 2]
        at += 2
    nm_ref, inner_ref, ggu_ref, gnf_ref, dout_ref = refs[at : at + 5]
    at += 5
    if near:
        mid_ref, mixed_ref = refs[at : at + 2]
        gnm_refs = refs[at + 2 : at + 2 + chips]
        lay_refs = refs[at + 2 + chips : at + 2 + 2 * chips]
        at += 2 + 2 * chips
    else:
        gnm_ref, lay_ref = refs[at : at + 2]
        at += 2
    w_s, wo_s, extra_s, sems = refs[at:]
    step = pl.program_id(0)
    rows = nm_ref.shape[0]

    @pl.when(step == 0)
    def _():
        copies = [
            pltpu.make_async_copy(part, extra_s.at[j], sems.at[j])
            for j, part in enumerate(extra_parts)
        ]
        for copy in copies:
            copy.start()
        assemble(w_s, wgu_ref)
        for j, copy in enumerate(copies):
            copy.wait()
            wo_s[j * WIDE : (j + 1) * WIDE, :] = extra_s[j, rows:, :]

    cat = jnp.concatenate([m[...] for m in mixed], axis=1)
    hidden = wd_ref.shape[0]
    middle = x_ref[:rows, :].astype(F32) + dot_nn(cat, wo_s[...])
    factor = rms_factor(middle)
    scaled = middle * factor
    nm = (scaled * nf_ref[...]).astype(BF16)
    nm_ref[...] = nm
    lin = dot_nn(nm, w_s[...])
    dout = extra_s[step if near else chips + step, :rows, :]
    dout_ref[...] = dout
    back = dot_nt(dout, wd_ref[...])
    gate, up = lin[:, :hidden], lin[:, hidden:]
    sig = jax.nn.sigmoid(gate)
    silu = gate * sig
    inner = (silu * up).astype(BF16)
    inner_ref[...] = inner
    g_gate = (back * up * (sig * (1.0 + gate * (1.0 - sig)))).astype(BF16)
    g_up = (back * silu).astype(BF16)
    ggu = jnp.concatenate([g_gate, g_up], axis=1)
    ggu_ref[...] = ggu
    gnm = dot_nt(ggu, w_s[...])
    lay = dot_nn(inner, wd_ref[...])

    @pl.when(step == 0)
    def _():
        gnf_ref[...] = jnp.zeros_like(gnf_ref)
        if near:
            mid_ref[...] = middle
            mixed_ref[...] = cat

    gnf_ref[...] += jnp.sum(gnm * scaled, axis=0, keepdims=True)
    if near:
        gnm = (gnm + got_ref[...].astype(F32)).astype(BF16)
        lay = (lay + lay_got_ref[...].astype(F32)).astype(BF16)
        for r in range(chips):

            @pl.when(step == r)
            def _(r=r):
                gnm_refs[r][...] = gnm
                lay_refs[r][...] = lay

    else:
        gnm_ref[...] = gnm.astype(BF16)
        lay_ref[...] = lay.astype(BF16)


def ffn(side, own_parts, sib_stack, x, near_extra, far_extra, wgu, wd, norm_ffn, got=()):
    chips = len(own_parts)
    rows, width = near_extra[0].shape
    rows -= WIDE
    half = rows * chips
    hidden = wd.shape[0]
    near = side == 0
    row_block = lambda cols: pl.BlockSpec((rows, cols), lambda i: (i, 0))
    piece = lambda r: pl.BlockSpec((rows, WIDE), lambda i: (i ^ r, 0))
    stack = lambda r: pl.BlockSpec((rows, WIDE), lambda i: (r * chips + (i ^ r), 0))
    out_shape = [
        shaped((half, width), BF16), shaped((half, hidden), BF16), shaped((half, 2 * hidden), BF16),
        shaped((1, width), F32), shaped((half, width), BF16),
    ]
    out_specs = [
        row_block(width), row_block(hidden), row_block(2 * hidden), whole(out_shape[3]),
        row_block(width),
    ]
    if near:
        more = [shaped((rows, width), F32), shaped((rows, 2 * chips * WIDE), BF16)]
        more += [shaped((rows, width), BF16)] * (2 * chips)
        out_shape += more
        out_specs += [whole(a) for a in more]
    else:
        out_shape += [shaped((half, width), BF16)] * 2
        out_specs += [row_block(width)] * 2
    return pl.pallas_call(
        functools.partial(ffn_kernel, chips=chips, near=near),
        grid=(chips,),
        in_specs=[piece(r) for r in range(chips)]
        + [stack(r) for r in range(chips)]
        + [ANY] * (2 * chips)
        + [pl.BlockSpec((rows + 16, width), lambda i: (i, 0))]
        + [whole(a) for a in (wgu, wd, norm_ffn)]
        + [row_block(width)] * len(got),
        out_specs=out_specs,
        out_shape=out_shape,
        scratch_shapes=[
            pltpu.VMEM((width, 2 * hidden), BF16),
            pltpu.VMEM((2 * chips * WIDE, width), BF16),
            pltpu.VMEM((2 * chips, rows + WIDE, width), BF16),
            pltpu.SemaphoreType.DMA((2 * chips,)),
        ],
        compiler_params=params(),
        cost_estimate=pl.CostEstimate(
            flops=2 * half * width * (2 * chips * WIDE + 6 * hidden),
            bytes_accessed=half * width * 12,
            transcendentals=half * hidden,
        ),
        name="ffn_half",
    )(
        *own_parts, *[sib_stack] * chips, *near_extra, *far_extra, x, wgu, wd, norm_ffn, *got,
    )


def ffn_grads_kernel(nm0, nm1, ggu0, ggu1, in0, in1, dout0, dout1, _, gu_ref, gd_ref):
    gu = dot_tn(nm0[...], ggu0[...]) + dot_tn(nm1[...], ggu1[...])
    gu = gu.astype(BF16)
    if len(gu_ref.shape) == 2:
        gu_ref[...] = gu
    else:
        z_count, parts, shard, _ = gu_ref.shape
        for f in range(z_count):
            for s in range(parts):
                at = (s * z_count + f) * shard
                gu_ref[f, s] = gu[at : at + shard]
    gd_ref[...] = (dot_tn(in0[...], dout0[...]) + dot_tn(in1[...], dout1[...])).astype(BF16)


def ffn_grads(nm, ggu, inner, dout, seq_count, z_count, ticket):
    half, width = nm[0].shape
    hidden = inner[0].shape[1]
    shard = width // (seq_count * z_count)
    steps = max(1, min(4, hidden // WIDE))
    column_block = lambda cols: pl.BlockSpec((half, cols // steps), lambda i: (0, i))
    if shard % 16 == 0 and seq_count % steps == 0:
        gu = shaped((z_count, seq_count, shard, 2 * hidden), BF16)
        gu_spec = pl.BlockSpec(
            (z_count, seq_count // steps, shard, 2 * hidden), lambda i: (0, i, 0, 0)
        )
    else:
        gu = shaped((width, 2 * hidden), BF16)
        gu_spec = pl.BlockSpec((width // steps, 2 * hidden), lambda i: (i, 0))
    gu, gd = pl.pallas_call(
        ffn_grads_kernel,
        grid=(steps,),
        in_specs=[column_block(width)] * 2
        + [whole(a) for a in ggu]
        + [column_block(hidden)] * 2
        + [whole(a) for a in dout]
        + [ANY],
        out_specs=[gu_spec, pl.BlockSpec((hidden // steps, width), lambda i: (i, 0))],
        out_shape=[gu, shaped((hidden, width), BF16)],
        compiler_params=params(),
        cost_estimate=pl.CostEstimate(
            flops=2 * half * width * 6 * hidden, bytes_accessed=half * width * 16, transcendentals=0
        ),
        name="ffn_grads",
    )(*nm, *ggu, *inner, *dout, ticket)
    if len(gu.shape) == 2:
        gu = gu.reshape(seq_count, z_count, shard, 2 * hidden).transpose(1, 0, 2, 3)
    return gu.reshape(width, 2 * hidden), gd


def pair_kernel(a0, a1, b0, b1, w_ref, _, out_ref, sum_ref):
    product = dot_tn(a0[...], b0[...]) + dot_tn(a1[...], b1[...])
    out_ref[...] = product.astype(BF16)
    rows = product.shape[0]
    if len(w_ref.shape) == 2:
        w = w_ref[...].astype(F32)
    else:
        w = w_ref[...].astype(F32)
        z_count, parts, shard, wide = w.shape
        w = jnp.concatenate([w[f, s] for s in range(parts) for f in range(z_count)], axis=0)
    total = jnp.sum(product * w, axis=1, keepdims=True) * jnp.ones((rows, WIDE), F32)
    sum_ref[...] = total.T[:8]


def pair_product(left, right, w, ticket, steps=4):
    half, width = left[0].shape
    wide = right[0].shape[1]
    if len(w.shape) == 2:
        w_spec = pl.BlockSpec((width // steps, wide), lambda i: (i, 0))
    else:
        block = (w.shape[0], w.shape[1] // steps) + w.shape[2:]
        w_spec = pl.BlockSpec(block, lambda i: (0, i, 0, 0))
    return pl.pallas_call(
        pair_kernel,
        grid=(steps,),
        in_specs=[pl.BlockSpec((half, width // steps), lambda i: (0, i))] * 2
        + [whole(a) for a in right]
        + [w_spec, ANY],
        out_specs=[
            pl.BlockSpec((width // steps, wide), lambda i: (i, 0)),
            pl.BlockSpec((8, width // steps), lambda i: (0, i)),
        ],
        out_shape=[shaped((width, wide), BF16), shaped((8, width), F32)],
        compiler_params=params(),
        cost_estimate=pl.CostEstimate(
            flops=4 * half * width * wide, bytes_accessed=half * width * 6, transcendentals=0
        ),
        name="pair_product",
    )(*left, *right, w, ticket)


def added(pieces):
    total = pieces[0][...].astype(F32)
    for piece in pieces[1:]:
        total = total + piece[...].astype(F32)
    return total


def norm_back(values, gain, incoming):
    factor = rms_factor(values)
    weighted = incoming * gain
    return factor * weighted - values * (factor * factor * factor) * jnp.mean(
        weighted * values, axis=-1, keepdims=True
    )


def middle_back_kernel(*refs, chips):
    extra = refs[chips : 3 * chips]
    mid_ref, nf_ref, me_ref, gm_ref, gb_ref, out_ref = refs[3 * chips :]
    rows = mid_ref.shape[0]
    grad = extra[0][:rows, :].astype(F32) + norm_back(mid_ref[...], nf_ref[...], added(refs[:chips]))
    gm_ref[...] = grad
    branch = grad.astype(BF16)
    gb_ref[...] = branch
    for side in range(2):
        for r in range(chips):
            part = dot_nt(branch, extra[side * chips + r][rows:, :])
            out_ref[me_ref[0] ^ (2 * r + side)] = part.astype(BF16)


def middle_back(pieces, middle, norm_ffn, near_extra, far_extra, me):
    chips = len(pieces)
    rows, width = middle.shape
    vmem = pl.BlockSpec(memory_space=pltpu.VMEM)
    return pl.pallas_call(
        functools.partial(middle_back_kernel, chips=chips),
        in_specs=[vmem] * (3 * chips + 2) + [pl.BlockSpec(memory_space=pltpu.SMEM)],
        out_shape=[
            shaped((rows, width), F32), shaped((rows, width), BF16),
            shaped((2 * chips, rows, WIDE), BF16),
        ],
        compiler_params=params(False),
        cost_estimate=pl.CostEstimate(
            flops=2 * rows * width * 2 * chips * WIDE,
            bytes_accessed=rows * width * 12,
            transcendentals=0,
        ),
        name="middle_back",
    )(*pieces, *near_extra, *far_extra, middle, norm_ffn, me)


def input_back_kernel(*refs, chips):
    x_ref, gm_ref, na_ref, out_ref = refs[chips:]
    out_ref[...] = gm_ref[...] + norm_back(x_ref[...].astype(F32), na_ref[...], added(refs[:chips]))


def input_back(pieces, x, grad_middle, norm_attn):
    return pl.pallas_call(
        functools.partial(input_back_kernel, chips=len(pieces)),
        out_shape=shaped(x.shape, F32),
        compiler_params=params(False),
        name="input_back",
    )(*pieces, x, grad_middle, norm_attn)


def project_back_kernel(*refs, head_size):
    dq, qlin, klin, lanes = refs[0:2], refs[2:4], refs[4:6], refs[6:8]
    dk_ref, dv_ref, qg_ref, kg_ref = refs[8:12]
    gl, gain_ref = refs[12:14], refs[14]
    half = head_size // 2
    rows = qlin[0].shape[0]
    lane = lanes_of((rows, WIDE))
    blocks = head_blocks(head_size)

    @pl.when(pl.program_id(0) == 0)
    def _():
        gain_ref[...] = jnp.zeros_like(gain_ref)

    for side in range(2):
        cosine, sine = tables(lanes[side][:half, :], lanes[side][half : 2 * half, :])

        def back(grad, u, gain, at):
            grad = grad.astype(F32)
            grad = grad * cosine - partner(grad, lane, head_size) * sine
            factor = lax.rsqrt(head_sum(u * u, blocks) * (1.0 / head_size) + EPSILON)
            gain_ref[at : at + 1, :] += jnp.sum(grad * u * factor, axis=0, keepdims=True)
            weighted = grad * gain
            mean = head_sum(weighted * u, blocks) * (1.0 / head_size)
            return (factor * weighted - u * (factor * factor * factor) * mean).astype(BF16)

        gq = back(dq[side][...], qlin[side][...], qg_ref[...], 0)
        gk = back(dk_ref[side], klin[side][...], kg_ref[...], 1)
        gl[side][...] = jnp.concatenate([gq, gk, dv_ref[side]], axis=1)


def project_back(dq, qlin, klin, lane_rows, dk, dv, q_gain, k_gain, head_size, chips):
    half = qlin[0].shape[0]
    rows = half // chips
    count = lane_rows[0].shape[0]
    row_block = lambda cols: pl.BlockSpec((rows, cols), lambda i: (i, 0))
    both = pl.BlockSpec((2, rows, WIDE), lambda i: (0, i, 0))
    gain = shaped((8, WIDE), F32)
    return pl.pallas_call(
        functools.partial(project_back_kernel, head_size=head_size),
        grid=(chips,),
        in_specs=[row_block(WIDE)] * 6
        + [pl.BlockSpec((count, rows), lambda i: (0, i))] * 2
        + [both, both, whole(q_gain), whole(k_gain)],
        out_specs=[row_block(3 * WIDE), row_block(3 * WIDE), whole(gain)],
        out_shape=[shaped((half, 3 * WIDE), BF16)] * 2 + [gain],
        compiler_params=params(),
        cost_estimate=pl.CostEstimate(
            flops=2 * half * WIDE * 16 * WIDE, bytes_accessed=half * WIDE * 40, transcendentals=0
        ),
        name="project_back",
    )(*dq, *qlin, *klin, *lane_rows, dk, dv, q_gain, k_gain)


def spread_back_kernel(*refs, chips, near):
    gl_ref, w_ref = refs[:2]
    got = refs[2:3] if near else ()
    outs, w_s = refs[2 + len(got) : -1], refs[-1]
    step = pl.program_id(0)

    @pl.when(step == 0)
    def _():
        assemble(w_s, w_ref)

    out = dot_nt(gl_ref[...], w_s[...])
    if near:
        out = (out + got[0][...].astype(F32)).astype(BF16)
        for r in range(chips):

            @pl.when(step == r)
            def _(r=r):
                outs[r][...] = out

    else:
        outs[0][...] = out.astype(BF16)


def spread_back(gl, w, chips, got=None):
    half, wide = gl.shape
    width = math.prod(w.shape[:-1])
    rows = half // chips
    near = got is not None
    row_block = lambda cols: pl.BlockSpec((rows, cols), lambda i: (i, 0))
    out_shape = [shaped((rows, width), BF16)] * chips if near else [shaped((half, width), BF16)]
    return pl.pallas_call(
        functools.partial(spread_back_kernel, chips=chips, near=near),
        grid=(chips,),
        in_specs=[row_block(wide), whole(w)] + ([row_block(width)] if near else []),
        out_specs=[whole(a) for a in out_shape] if near else [row_block(width)],
        out_shape=out_shape,
        scratch_shapes=[pltpu.VMEM((width, wide), BF16)],
        compiler_params=params(),
        cost_estimate=pl.CostEstimate(
            flops=2 * half * width * wide, bytes_accessed=half * width * 4, transcendentals=0
        ),
        name="spread_back",
    )(gl, w, *([got] if near else []))


def last_kernel(in_ref, *refs, z_count, shard):
    outs, small_ref = refs[:-1], refs[-1]
    seq_count = in_ref.shape[0] // z_count
    small = None
    for s in range(seq_count):
        total = None
        for f in range(z_count):
            block = in_ref[s * z_count + f].astype(F32)
            total = block if total is None else total + block
        for i, out_ref in enumerate(outs):
            out_ref[:, s * WIDE : (s + 1) * WIDE] = total[:shard, i * WIDE : (i + 1) * WIDE]
        small = total[shard:] if small is None else small + total[shard:]
    small_ref[...] = small


def last_sums(blocks, z_count, shard):
    count, rows, wide = blocks.shape
    seq_count = count // z_count
    return pl.pallas_call(
        functools.partial(last_kernel, z_count=z_count, shard=shard),
        out_shape=[shaped((shard, seq_count * WIDE), F32)] * 3 + [shaped((rows - shard, wide), F32)],
        compiler_params=params(False),
        name="last_sums",
    )(blocks)


def swap(x, seq_count, bits):
    return lax.ppermute(x, "seq", [(i, i ^ bits) for i in range(seq_count)])


def to_chips(x, seq_count):
    return [x] + [swap(x, seq_count, 2 * r) for r in range(1, seq_count // 2)]


def spread_slots(slots, seq_count):
    return [slots[0]] + [swap(slots[r], seq_count, 2 * r) for r in range(1, len(slots))]


def after(values, *others):
    kept, _ = lax.optimization_barrier((values, others))
    return kept


def add_up(parts):
    total = parts[0].astype(F32)
    for part in parts[1:]:
        total = total + part.astype(F32)
    return total


def body(
    tokens, weight_query, weight_key, weight_value, weight_out, weight_gate, weight_up, weight_down,
    norm_attn, norm_ffn, query_gain, key_gain, variate_bias, variate_ids, sample_ids, time_ids,
    out_grad,
):
    seq_count = lax.axis_size("seq")
    z_count = lax.axis_size("fsdp")
    everyone = seq_count * z_count
    chips = seq_count // 2
    _, rows, width = tokens.shape
    heads = variate_bias.shape[1]
    head_size = query_gain.shape[0]
    half_size = head_size // 2
    shard = weight_query.shape[0]
    features = heads * head_size
    hidden = weight_gate.shape[1] // seq_count
    me = lax.axis_index("seq")
    x_own = tokens.reshape(rows, width)
    dout_own = out_grad.reshape(rows, width)

    columns = columns_by_device(
        (weight_query, weight_key, weight_value, weight_gate, weight_up), seq_count
    )
    columns = lax.all_to_all(columns, "seq", split_axis=0, concat_axis=0, tiled=True)
    w_out_rows = lax.all_gather(weight_out, "fsdp", axis=0, tiled=True)
    columns = after(columns, w_out_rows)
    w_qkv = jnp.broadcast_to(
        columns[None, :, :, : 3 * WIDE], (z_count, seq_count, shard, 3 * WIDE)
    )
    w_qkv = gathered(lax.all_to_all(w_qkv, "fsdp", split_axis=0, concat_axis=0, tiled=True))
    w_down = lax.all_gather(weight_down, "fsdp", axis=0, tiled=True)
    if features < WIDE:
        w_out_rows = jnp.pad(w_out_rows, ((0, WIDE - features), (0, 0)))
    w_gu = gathered(lax.all_gather(columns[:, :, 3 * WIDE :], "fsdp", axis=0, tiled=False))

    ids = jnp.concatenate([variate_ids, sample_ids, time_ids // 64, time_ids % 64], axis=0)
    ids = jnp.pad(ids.astype(BF16), ((0, 12), (0, width - rows)))
    packed = after(jnp.concatenate([x_own, ids], axis=0), columns, w_out_rows)
    near_x = to_chips(packed, seq_count)
    stack_x = jnp.concatenate(after(near_x, w_qkv), axis=0)
    far_x = swap(stack_x, seq_count, 1)
    extra = after(jnp.concatenate([dout_own, w_out_rows], axis=0), near_x[1:])
    near_extra = to_chips(extra, seq_count)
    far_extra = [swap(e, seq_count, 1) for e in near_extra]

    gain_attn = norm_attn.reshape(1, width)
    gain_ffn = norm_ffn.reshape(1, width)
    q_gain = jnp.tile(query_gain, WIDE // head_size).reshape(1, WIDE)
    k_gain = jnp.tile(key_gain, WIDE // head_size).reshape(1, WIDE)
    frequency = (10000.0 ** (-2.0 * jnp.arange(half_size).astype(F32) / head_size))[:, None]

    def projected(x):
        return project(
            x, chips, w_qkv, gain_attn, q_gain, k_gain, frequency, variate_bias, head_size
        )

    near_all = projected(stack_x)
    far_all = projected(far_x)
    nin, q_lin, k_lin, lane_rows, q_aug, k_aug, k_trans, v_aug = zip(near_all, far_all)
    attend_near = attend(q_aug[0], k_aug, v_aug, head_size)
    attend_far = attend(after(q_aug[1], attend_near, near_extra[1:3]), k_aug, v_aug, head_size)
    mixed, o_full, z_inverse = zip(attend_near, attend_far)
    own_parts = [to_chips(mixed[side], seq_count) for side in (0, 1)]
    own_parts[0] = after(own_parts[0], attend_far)
    sib_stack = [swap(jnp.concatenate(own_parts[side], axis=0), seq_count, 1) for side in (0, 1)]

    nm_far, inner_far, ggu_far, gnf_far, dout_far, gnm_far, lay_far = ffn(
        1, own_parts[1], sib_stack[0], far_x, near_extra, far_extra, w_gu, w_down, gain_ffn
    )
    nm_near, inner_near, ggu_near, gnf_near, dout_near, middle, mixed_own, *slots = ffn(
        0, own_parts[0], sib_stack[1], stack_x, near_extra, far_extra, w_gu, w_down, gain_ffn,
        (swap(gnm_far, seq_count, 1), swap(lay_far, seq_count, 1)),
    )

    gnm_parts = spread_slots(slots[:chips], seq_count)
    grad_gu, grad_down = ffn_grads(
        (nm_near, nm_far), (ggu_near, ggu_far), (inner_near, inner_far), (dout_near, dout_far),
        seq_count, z_count, swap(gnf_near, seq_count, 1),
    )
    me_row = jnp.reshape(me, (1,))
    grad_middle, grad_branch, g_out = middle_back(
        after(gnm_parts, grad_gu, grad_down),
        middle, gain_ffn, near_extra, far_extra, me_row,
    )
    g_all = lax.all_to_all(g_out, "seq", split_axis=0, concat_axis=0, tiled=True)

    grad_gu = lax.psum_scatter(grad_gu, "fsdp", scatter_dimension=0, tiled=True)
    grad_gu = grad_gu.reshape(seq_count, shard, 2 * hidden)
    grad_down = lax.psum_scatter(grad_down, "fsdp", scatter_dimension=0, tiled=True)
    grad_out = dot_tn(mixed_own, grad_branch).astype(BF16)
    half_out = chips * WIDE
    out_slots = add_up([grad_out[:half_out], swap(grad_out[half_out:], seq_count, 1)])
    out_slots = out_slots.astype(BF16)
    both_slots = [
        jnp.concatenate([slots[chips + r], out_slots[r * WIDE : (r + 1) * WIDE]], axis=0)
        for r in range(chips)
    ]
    both_parts = spread_slots(after(both_slots, g_all), seq_count)
    gu_got = lax.all_to_all(
        after(grad_gu, g_all), "seq", split_axis=0, concat_axis=0, tiled=True
    )

    dq_near, dq_far, dk, dv, bias_rows = attend_back(
        me_row, after(g_all, both_slots),
        q_aug, o_full, z_inverse, lane_rows, k_aug, k_trans, v_aug, head_size,
    )
    dq_far = after(dq_far, grad_gu, both_parts)
    gl_near, gl_far, gain_rows = project_back(
        (dq_near, dq_far), q_lin, k_lin, lane_rows, dk, dv, q_gain, k_gain, head_size, chips
    )
    (gni_far,) = spread_back(gl_far, w_qkv, chips)
    gni_got = swap(gni_far, seq_count, 1)
    grad_qkv, gna = pair_product(
        nin, (gl_near, gl_far), w_qkv, swap(gain_rows, seq_count, 1)
    )
    gni_slots = spread_back(
        gl_near, w_qkv, chips, after(gni_got, grad_qkv)
    )
    gni_parts = spread_slots(gni_slots, seq_count)
    both = add_up(after(both_parts, gni_slots))
    grad_out = both[rows : rows + features].astype(BF16)
    z_me = lax.axis_index("fsdp")
    z_parts = []
    for r in range(z_count):
        part = lax.dynamic_slice(grad_out, ((z_me ^ r) * shard, 0), (shard, width))
        if r:
            part = lax.ppermute(part, "fsdp", [(i, i ^ r) for i in range(z_count)])
        z_parts.append(part)
    grad_out = add_up(z_parts)
    in_grad = input_back(gni_parts, x_own, grad_middle, gain_attn)

    grad_qk_gain = gain_rows[:2, :features].reshape(2, heads, head_size).sum(axis=1)
    bias_cols = jnp.sum(bias_rows, axis=1).reshape(2, 2, 4).sum(axis=2)[:, :heads]
    bias_both = jnp.stack([bias_cols[0], bias_cols[1] - bias_cols[0]])
    bias_all = lax.dynamic_update_slice(
        jnp.zeros((2, heads * seq_count), F32), bias_both, (0, me * heads)
    )
    small = jnp.concatenate(
        [
            gna[0] / norm_attn,
            (gnf_near + gnf_far).reshape(-1),
            grad_qk_gain.reshape(-1),
            bias_all.reshape(-1),
        ]
    )
    count = small.shape[0]
    small_rows = -(-count // (8 * 3 * WIDE)) * 8
    small = jnp.pad(small, (0, small_rows * 3 * WIDE - count)).astype(BF16)
    small = jnp.broadcast_to(small.reshape(1, small_rows, 3 * WIDE), (everyone, small_rows, 3 * WIDE))
    grad_qkv = after(grad_qkv, gu_got, gni_slots)
    blocks = jnp.concatenate([grad_qkv.reshape(everyone, shard, 3 * WIDE), small], axis=1)
    last = lax.all_to_all(blocks, ("seq", "fsdp"), split_axis=0, concat_axis=0, tiled=True)
    gu_got = after(gu_got, blocks)
    grad_down = after(grad_down, gni_parts[3:])
    layer_out = (middle + both[:rows]).astype(BF16)
    grad_gu = gu_got.transpose(1, 0, 2).astype(F32)
    grad_gate = grad_gu[:, :, :hidden].reshape(shard, seq_count * hidden)
    grad_up = grad_gu[:, :, hidden:].reshape(shard, seq_count * hidden)
    grad_down = grad_down.astype(F32)
    *grad_qkv, small = last_sums(last, z_count, shard)
    grad_query, grad_key, grad_value = (
        g.reshape(shard, seq_count, WIDE)[:, :, :features].reshape(shard, width)
        if features < WIDE
        else g
        for g in grad_qkv
    )
    small = small.reshape(-1)
    cut = 2 * width + 2 * head_size
    grad_bias = lax.dynamic_slice(
        small[cut:count].reshape(2, heads * seq_count), (0, me * heads), (2, heads)
    )
    return (
        layer_out.reshape(tokens.shape),
        in_grad.reshape(tokens.shape),
        grad_query,
        grad_key,
        grad_value,
        grad_out,
        grad_gate,
        grad_up,
        grad_down,
        small[:width],
        small[width : 2 * width],
        small[2 * width : 2 * width + head_size],
        small[2 * width + head_size : cut],
        grad_bias,
    )


def solution(mesh):
    rows = P("fsdp", "seq", None)
    shards = P(("seq", "fsdp"), None)
    ids = P("fsdp", "seq")
    bias = P(None, "seq")
    return jax.shard_map(
        body,
        mesh=mesh,
        in_specs=(rows,) + (shards,) * 7 + (P(),) * 4 + (bias, ids, ids, ids, rows),
        out_specs=(rows, rows) + (shards,) * 7 + (P(),) * 4 + (bias,),
        check_vma=False,
    )
```

time: 472 us -> 370 us (0.78)
  blocking collectives: 91.8 us -> 14.3 us
  Pallas kernels: 120 us -> 150 us
  local copies, waits for them, and re-layouts: 52.9 us -> 24.8 us
  matrix products: 20.7 us -> 1.78 us
  other arithmetic: 32.4 us -> 14.9 us
  waiting for transfers between devices: 74.9 us -> 84.4 us
  starting transfers between devices: 58.4 us -> 63.4 us
    psum x1 -> x0, blocking collectives: 47.7 us -> none  [body(): small = lax.psum(small, ('seq', 'fsdp'))]
    pallas_call x8 -> x14, Pallas kernels: 101 us -> 133 us  [the longest x2 42 us: ffn(): pl.pallas_call(functools.partial(ffn_kernel, chips=chips, near=near), gri...]
    all_gather x1, blocking collectives: 44 us -> 14.3 us  [body(): w_out_rows = lax.all_gather(weight_out, 'fsdp', axis=0, tiled=True)]
    dot_general x7 -> x1, matrix products: 20.7 us -> 1.78 us  [dot_tn(): lax.dot_general(left, right, (((0,), (0,)), ((), ())), preferred_element_...]
    ppermute x0 -> x3, waiting for transfers between devices: none -> 13.3 us  [body(): part = lax.ppermute(part, 'fsdp', [(i, i ^ r) for i in range(z_count)])]
    ppermute x40 -> x34, waiting for transfers between devices: 74.8 us -> 64.8 us  [swap(): return lax.ppermute(x, 'seq', [(i, i ^ bits) for i in range(seq_count)])]
    convert_element_type x8 -> x3, other arithmetic: 12.3 us -> 2.29 us  [the longest x1 1.79 us: body(): grad_down = grad_down.astype(F32)]
    unnamed x138 -> x104, local copies, waits for them, and re-layouts: 21 us -> 12.7 us
  transfers between devices with their start and end apart: 48 -> 46, of which waited for: 14 -> 12; matrix products, arithmetic and copies ran while one was open for 21% -> 7% of each run, Pallas kernels for 26% -> 25%
where the time goes in v2:
time: 370 us; the launch traced here: 368 us
  Pallas kernels  150 us (41%)
  waiting for transfers between devices  84.4 us (23%)
  starting transfers between devices  63.4 us (17%)
  local copies, waits for them, and re-layouts  24.8 us (7%)
  other arithmetic  14.9 us (4%)
  between operations  14.5 us (4%)
  blocking collectives  14.3 us (4%)
    ppermute x34, waiting for transfers between devices, swap(): return lax.ppermute(x, 'seq', [(i, i ^ bits) for i in range(seq_count)])  64.8 us
    pallas_call x2, Pallas kernels, ffn(): pl.pallas_call(functools.partial(ffn_kernel, chips=chips, near=near), gri...  42 us
    ppermute x34, starting transfers between devices, swap(): return lax.ppermute(x, 'seq', [(i, i ^ bits) for i in range(seq_count)])  31.2 us
    pallas_call x1, Pallas kernels, attend_back(): pl.pallas_call(functools.partial(attend_back_kernel, chips=chips, heads=h...  26.8 us
    pallas_call x2, Pallas kernels, attend(): pl.pallas_call(functools.partial(attend_kernel, heads=heads, head_size=he...  17.2 us
    pallas_call x2, Pallas kernels, project(): pl.pallas_call(functools.partial(project_kernel, heads=heads, head_size=h...  14.4 us
    all_gather x1, blocking collectives, body(): w_out_rows = lax.all_gather(weight_out, 'fsdp', axis=0, tiled=True)  14.3 us
    ppermute x3, waiting for transfers between devices, body(): part = lax.ppermute(part, 'fsdp', [(i, i ^ r) for i in range(z_count)])  13.3 us
  transfers between devices with their start and end apart: 46, of which 12 were waited for; matrix products, arithmetic and copies ran while one was open for 7% of the time, Pallas kernels for 25%

profile of v2, /device:TPU:0, one launch (start us, length us, event | category | flops | bytes accessed | tf_op | source)
XLA Modules:
  0.0 368.0 jit_solution(8707436479360209866)
XLA Ops:
  14.7 14.3 %all_gather.12 = bf16[128,1024]{1,0:T(8,128)(2,1)S(1)} all-gather(bf16[32,1024]{1,0:T(8,128)(2,1)S(1)} %copy-done.35), channel_id=1, replica_groups=mesh['seq'=8,'fsdp'=4] {'fsdp'}, dimensions={0}, use_global_device_ids=true | all-gather | bytes 327680 | tf_op jit(solution)/shard_map/all_gather | solution.py:850
  39.0 12.0 %collective-permute-done = bf16[272,1024]{1,0:T(8,128)(2,1)S(1)} collective-permute-done((bf16[272,1024]{1,0:T(8,128)(2,1)S(1)}, bf16[272,1024]{1,0:T(8,128)(2,1)S(1)}, u32[]{:S(2)}, u32[]{:S(2)}) %collective-permute-start) | collective-permute-done | bytes 557088 | tf_op jit(solution)/shard_map/ppermute | solution.py:803
  51.0 9.3 %collective-permute-done.1 = bf16[272,1024]{1,0:T(8,128)(2,1)S(1)} collective-permute-done((bf16[272,1024]{1,0:T(8,128)(2,1)S(1)}, bf16[272,1024]{1,0:T(8,128)(2,1)S(1)}, u32[]{:S(2)}, u32[]{:S(2)}) %collective-permute-start.1) | collective-permute-done | bytes 557088 | tf_op jit(solution)/shard_map/ppermute | solution.py:803
  73.5 7.2 %project.2 = (bf16[1024,1024]{1,0:T(8,128)(2,1)}, f32[1024,128]{1,0:T(8,128)}, f32[1024,128]{1,0:T(8,128)}, f32[72,1024]{1,0:T(8,128)}, bf16[1024,256]{1,0:T(8,1...) custom-call(bf16[1088,1024]{1,0:T(8,128)(2,1)} %copy-done.3, ...), custom_call_target="tpu_custom_call" | custom-call | flops 805306368 | bytes 8388608 | tf_op jit(solution)/shard_map/project/pallas_call | solution.py:219
  80.7 7.2 %project.3 = (bf16[1024,1024]{1,0:T(8,128)(2,1)}, f32[1024,128]{1,0:T(8,128)}, f32[1024,128]{1,0:T(8,128)}, f32[72,1024]{1,0:T(8,128)}, bf16[1024,256]{1,0:T(8,1...) custom-call(bf16[1088,1024]{1,0:T(8,128)(2,1)} %collective-permute-done.3.x_re, ...), custom_call_target="tpu_custom_call" | custom-call | flops 805306368 | bytes 8388608 | tf_op jit(solution)/shard_map/project/pallas_call | solution.py:219
  87.9 8.6 %attend.2 = (bf16[1024,128]{1,0:T(8,128)(2,1)}, f32[1024,128]{1,0:T(8,128)}, f32[1024,128]{1,0:T(8,128)}) custom-call(bf16[1024,256]{1,0:T(8,128)(2,1)} %get-tuple-element.118.qa_ref.refs_2_, bf16[2,1024,256]{2,1,0:T(8,128)(2,1)} %get-tuple-element.119.ka0.refs_10_, bf16[2,1024,256]{2,1,0:T(8,128)(2,1)} %get-tuple-element.120.ka1.refs_11_, ...), custom_call_target="tpu_custom_call" | custom-call | flops 4294967296 | bytes 4194304 | tf_op jit(solution)/shard_map/attend/pallas_call | solution.py:273
  103.1 5.4 %collective-permute-start.6 = (bf16[1024,128]{1,0:T(8,128)(2,1)}, bf16[1024,128]{1,0:T(8,128)(2,1)S(1)}, u32[]{:S(2)}, u32[]{:S(2)}) collective-permute-start(bf16[1024,128]{1,0:T(8,128)(2,1)} %get-tuple-element.132.refs_0_), channel_id=1, source_target_pairs={{0,24},{4,28},{8,16},{12,20},{16,8},{20,12},{24,0},{28,4},{1,25},{... | collective-permute-start | bytes 786440 | tf_op jit(solution)/shard_map/ppermute | solution.py:803
  108.5 8.6 %attend.3 = (bf16[1024,128]{1,0:T(8,128)(2,1)}, f32[1024,128]{1,0:T(8,128)}, f32[1024,128]{1,0:T(8,128)}) custom-call(bf16[1024,256]{1,0:T(8,128)(2,1)} %get-tuple-element.128.qa_ref.refs_3_, bf16[2,1024,256]{2,1,0:T(8,128)(2,1)} %get-tuple-element.119.ka0.refs_10_, bf16[2,1024,256]{2,1,0:T(8,128)(2,1)} %get-tuple-element.120.ka1.refs_11_, ...), custom_call_target="tpu_custom_call" | custom-call | flops 4294967296 | bytes 4194304 | tf_op jit(solution)/shard_map/attend/pallas_call | solution.py:273
  123.7 10.5 %collective-permute-done.10.refs_2_ = bf16[1024,128]{1,0:T(8,128)(2,1)S(1)} collective-permute-done((bf16[1024,128]{1,0:T(8,128)(2,1)}, bf16[1024,128]{1,0:T(8,128)(2,1)S(1)}, u32[]{:S(2)}, u32[]{:S(2)}) %collective-permute-start.10) | collective-permute-done | bytes 262176 | tf_op jit(solution)/shard_map/ppermute | solution.py:803
  136.2 19.1 %ffn_half.2 = (bf16[1024,1024]{1,0:T(8,128)(2,1)}, bf16[1024,512]{1,0:T(8,128)(2,1)}, bf16[1024,1024]{1,0:T(8,128)(2,1)}, f32[1,1024]{1,0:T(1,128)}, bf16[1024,1...) custom-call(bf16[1024,128]{1,0:T(8,128)(2,1)} %get-tuple-element.129.refs_0_, ...), custom_call_target="tpu_custom_call" | custom-call | flops 8589934592 | bytes 12582912 | tf_op jit(solution)/shard_map/ffn_half/pallas_call | solution.py:495
  157.3 6.7 %collective-permute-done.12.refs_4_.refs_5_.refs_6_.refs_7_ = bf16[4096,128]{1,0:T(8,128)(2,1)S(1)} collective-permute-done((bf16[4096,128]{1,0:T(8,128)(2,1)S(1)}, bf16[4096,128]{1,0:T(8,128)(2,1)S(1)}, u32[]{:S(2)}, u32[]{:S(2)}) %collective-permute-start.12) | collective-permute-done | bytes 1048608 | tf_op jit(solution)/shard_map/ppermute | solution.py:803
  165.8 22.9 %ffn_half.3 = (bf16[1024,1024]{1,0:T(8,128)(2,1)}, bf16[1024,512]{1,0:T(8,128)(2,1)}, bf16[1024,1024]{1,0:T(8,128)(2,1)}, f32[1,1024]{1,0:T(1,128)}, bf16[1024,1...) custom-call(bf16[1024,128]{1,0:T(8,128)(2,1)} %get-tuple-element.132, ...), custom_call_target="tpu_custom_call" | custom-call | flops 8589934592 | bytes 12582912 | tf_op jit(solution)/shard_map/ffn_half/pallas_call | solution.py:495
  193.0 12.5 %ffn_grads.1 = (bf16[4,8,32,1024]{3,2,1,0:T(8,128)(2,1)}, bf16[512,1024]{1,0:T(8,128)(2,1)}) custom-call(bf16[1024,1024]{1,0:T(8,128)(2,1)} %get-tuple-element.145.nm0, bf16[1024,1024]{1,0:T(8,128)(2,1)} %get-tuple-element.146.nm1, bf16[1024,1024]{1,0:T(8,128)(2,1)} %get-tuple-element.147.ggu0, bf16[1024,1024]{1,0:T(8,128)(2,1)} %get-tuple-element.148.ggu1, ...), custom_call_target="tpu_custom_call" | custom-call | flops 6442450944 | bytes 16777216 | tf_op jit(solution)/shard_map/ffn_grads/pallas_call | solution.py:552
  205.6 9.0 %collective-permute-done.22.refs_2_ = bf16[256,1024]{1,0:T(8,128)(2,1)S(1)} collective-permute-done((bf16[256,1024]{1,0:T(8,128)(2,1)}, bf16[256,1024]{1,0:T(8,128)(2,1)S(1)}, u32[]{:S(2)}, u32[]{:S(2)}) %collective-permute-start.22) | collective-permute-done | bytes 524320 | tf_op jit(solution)/shard_map/ppermute | solution.py:803
  215.6 6.5 %middle_back.1 = (f32[256,1024]{1,0:T(8,128)}, bf16[256,1024]{1,0:T(8,128)(2,1)}, bf16[8,256,128]{2,1,0:T(8,128)(2,1)}) custom-call(bf16[256,1024]{1,0:T(8,128)(2,1)} %get-tuple-element.156.refs_0_, bf16[256,1024]{1,0:T(8,128)(2,1)} %copy-done.20, bf16[256,1024]{1,0:T(8,128)(2,1)} %copy-done.21, bf16[256,1024]{1,0:T(8,128)(2,1)} %copy-done.22, ...), custom_call_target="tpu_custom_call" | custom-call | flops 536870912 | bytes 3145728 | tf_op jit(solution)/shard_map/middle_back/pallas_call | solution.py:647
  232.7 6.2 %all-to-all-done.2.refs_1_ = bf16[8,256,128]{2,1,0:T(8,128)(2,1)} async-done(((bf16[8,256,128]{2,1,0:T(8,128)(2,1)}), bf16[8,256,128]{2,1,0:T(8,128)(2,1)}, u32[]{:S(2)}, u32[]{:S(2)}) %all-to-all-start.2) | async-done | bytes 524320 | tf_op jit(solution)/shard_map/all_to_all | solution.py:910
  242.4 26.8 %attend_back.1 = (bf16[1024,128]{1,0:T(8,128)(2,1)}, bf16[1024,128]{1,0:T(8,128)(2,1)}, bf16[2,1024,128]{2,1,0:T(8,128)(2,1)}, bf16[2,1024,128]{2,1,0:T(8,128)(2,1)}, f32[16,256]{1,0:T(8,128)}) custom-call(s32[1]{0:T(128)} %bitcast.6.refs_14_.refs_0_, bf16[8,256,128]{2,1,0:T(8,128)(2,1)} %all-to-all-done.2.refs_1_, ...), custom_call_target="tpu_custom_call" | custom-call | flops 17179869184 | bytes 8388608 | tf_op jit(solution)/shard_map/attend_back/pallas_call | solution.py:359
  269.2 6.5 %collective-permute-done.27 = bf16[384,1024]{1,0:T(8,128)(2,1)S(1)} collective-permute-done((bf16[384,1024]{1,0:T(8,128)(2,1)}, bf16[384,1024]{1,0:T(8,128)(2,1)S(1)}, u32[]{:S(2)}, u32[]{:S(2)}) %collective-permute-start.27) | collective-permute-done | bytes 786464 | tf_op jit(solution)/shard_map/ppermute | solution.py:803
  275.8 6.1 %project_back.1 = (bf16[1024,384]{1,0:T(8,128)(2,1)}, bf16[1024,384]{1,0:T(8,128)(2,1)}, f32[8,128]{1,0:T(8,128)}) custom-call(bf16[1024,128]{1,0:T(8,128)(2,1)} %get-tuple-element.174.refs_0_, bf16[1024,128]{1,0:T(8,128)(2,1)} %get-tuple-element.176.refs_1_, f32[1024,128]{1,0:T(8,128)} %get-tuple-element.177.refs_2_, ...), custom_call_target="tpu_custom_call" | custom-call | flops 536870912 | bytes 5242880 | tf_op jit(solution)/shard_map/project_back/pallas_call | solution.py:715
  292.3 6.4 %pair_product.1 = (bf16[1024,384]{1,0:T(8,128)(2,1)}, f32[8,1024]{1,0:T(8,128)}) custom-call(bf16[1024,1024]{1,0:T(8,128)(2,1)} %get-tuple-element.185.a0, bf16[1024,1024]{1,0:T(8,128)(2,1)} %get-tuple-element.186.a1, bf16[1024,384]{1,0:T(8,128)(2,1)} %get-tuple-element.183.b0.refs_0_, bf16[1024,384]{1,0:T(8,128)(2,1)} %get-tuple-element.184.refs_0_.b1, ...), custom_call_target="tpu_custom_call" | custom-call | flops 1610612736 | bytes 6291456 | tf_op jit(solution)/shard_map/pair_product/pallas_call | solution.py:595
  300.8 5.7 %spread_back.3 = (bf16[256,1024]{1,0:T(8,128)(2,1)}, bf16[256,1024]{1,0:T(8,128)(2,1)}, bf16[256,1024]{1,0:T(8,128)(2,1)}, bf16[256,1024]{1,0:T(8,128)(2,1)}) custom-call(bf16[1024,384]{1,0:T(8,128)(2,1)} %get-tuple-element.183.b0.refs_0_, bf16[4,8,32,384]{3,2,1,0:T(8,128)(2,1)} %copy-done, bf16[1024,1024]{1,0:T(8,128)(2,1)} %copy-done.7), custom_call_target="tpu_custom_call" | custom-call | flops 805306368 | bytes 4194304 | tf_op jit(solution)/shard_map/spread_back/pallas_call | solution.py:761
  308.7 6.4 %all-to-all-start.4 = ((bf16[32,40,384]{2,1,0:T(8,128)(2,1)}), bf16[32,40,384]{2,1,0:T(8,128)(2,1)S(1)}, u32[]{:S(2)}, u32[]{:S(2)}) async-start(bf16[32,40,384]{2,1,0:T(8,128)(2,1)} %pad_maximum_fusion.2), calls=%async_computation.5 | async-start | bytes 1966080 | tf_op jit(solution)/shard_map/all_to_all | solution.py:977
  325.8 7.5 %collective-permute-done.34 = bf16[32,1024]{1,0:T(8,128)(2,1)S(1)} collective-permute-done((bf16[32,1024]{1,0:T(8,128)(2,1)S(1)}, bf16[32,1024]{1,0:T(8,128)(2,1)S(1)}, u32[]{:S(2)}, u32[]{:S(2)}) %collective-permute-start.34) | collective-permute-done | bytes 65568 | tf_op jit(solution)/shard_map/ppermute | solution.py:952
  338.5 5.8 %collective-permute-done.35 = bf16[32,1024]{1,0:T(8,128)(2,1)S(1)} collective-permute-done((bf16[32,1024]{1,0:T(8,128)(2,1)S(1)}, bf16[32,1024]{1,0:T(8,128)(2,1)S(1)}, u32[]{:S(2)}, u32[]{:S(2)}) %collective-permute-start.35) | collective-permute-done | bytes 65568 | tf_op jit(solution)/shard_map/ppermute | solution.py:952
  (251 shorter events, 116.4 us)
Async XLA Ops:
  9.3 19.6 %all-to-all-start = ((bf16[8,32,1408]{2,1,0:T(8,128)(2,1)}), bf16[8,32,1408]{2,1,0:T(8,128)(2,1)S(1)}, u32[]{:S(2)}, u32[]{:S(2)}) async-start(bf16[8,32,1408]{2,1,0:T(8,128)(2,1)} %columns.1), calls=%async_computation | async-start | bytes 1441792 | tf_op jit(solution)/shard_map/all_to_all | solution.py:849
  30.1 31.9 %all-to-all-start.1 = ((bf16[4,8,32,384]{3,2,1,0:T(8,128)(2,1)}), bf16[4,8,32,384]{3,2,1,0:T(8,128)(2,1)S(1)}, u32[]{:S(2)}, u32[]{:S(2)}) async-start(bf16[4,8,32,384]{3,2,1,0:T(8,128)(2,1)} %broadcast_in_dim.8), calls=%async_computation.1 | async-start | bytes 1572864 | tf_op jit(solution)/shard_map/all_to_all | solution.py:855
  35.2 88.4 %all-gather.4.cloned.1.call-start = ((), (), s32[]{:S(2)}) async-start(), calls=%async_computation.7 | async-start | bytes 1310720 | tf_op jit(solution)/shard_map/all_gather | solution.py:856
  37.2 23.1 %collective-permute-start.1 = (bf16[272,1024]{1,0:T(8,128)(2,1)S(1)}, bf16[272,1024]{1,0:T(8,128)(2,1)S(1)}, u32[]{:S(2)}, u32[]{:S(2)}) collective-permute-start(bf16[272,1024]{1,0:T(8,128)(2,1)S(1)} %pad_maximum_fusion.8), channel_id=1, source_target_pairs={{0,16},{4,20},{8,24},{12,28},{16,0},{20,4},{24,8},{28,12},{1,17},{... | collective-permute-start | bytes 1671176 | tf_op jit(solution)/shard_map/ppermute | solution.py:803
  38.7 21.6 %collective-permute-start.2 = (bf16[272,1024]{1,0:T(8,128)(2,1)S(1)}, bf16[272,1024]{1,0:T(8,128)(2,1)S(1)}, u32[]{:S(2)}, u32[]{:S(2)}) collective-permute-start(bf16[272,1024]{1,0:T(8,128)(2,1)S(1)} %pad_maximum_fusion.8), channel_id=1, source_target_pairs={{0,24},{4,28},{8,16},{12,20},{16,8},{20,12},{24,0},{28,4},{1,25},{... | collective-permute-start | bytes 1671176 | tf_op jit(solution)/shard_map/ppermute | solution.py:803
  38.9 84.8 %all-gather.6.cloned.1.call-start = ((), (), s32[]{:S(2)}) async-start(), calls=%async_computation.10 | async-start | bytes 2621440 | tf_op jit(solution)/shard_map/all_gather | solution.py:859
  67.0 208.8 %reduce-scatter.3.cloned.1.call-start = ((), (), s32[]{:S(2)}) async-start(), calls=%async_computation.8 | async-start | bytes 2621440 | tf_op jit(solution)/shard_map/reduce_scatter | solution.py:912
  68.1 28.7 %collective-permute-start.7 = (bf16[384,1024]{1,0:T(8,128)(2,1)S(1)}, bf16[384,1024]{1,0:T(8,128)(2,1)}, u32[]{:S(2)}, u32[]{:S(2)}) collective-permute-start(bf16[384,1024]{1,0:T(8,128)(2,1)S(1)} %pad_maximum_fusion.3.refs_8_.refs_4_), channel_id=1, source_target_pairs={{0,8},{4,12},{8,0},{12,4},{16,24},{20,28},{24,16},{28,20},{1,9},{5... | collective-permute-start | bytes 2359304 | tf_op jit(solution)/shard_map/ppermute | solution.py:803
  68.6 34.6 %collective-permute-start.8 = (bf16[384,1024]{1,0:T(8,128)(2,1)S(1)}, bf16[384,1024]{1,0:T(8,128)(2,1)}, u32[]{:S(2)}, u32[]{:S(2)}) collective-permute-start(bf16[384,1024]{1,0:T(8,128)(2,1)S(1)} %pad_maximum_fusion.3.refs_8_.refs_4_), channel_id=1, source_target_pairs={{0,16},{4,20},{8,24},{12,28},{16,0},{20,4},{24,8},{28,12},{1,17},{... | collective-permute-start | bytes 2359304 | tf_op jit(solution)/shard_map/ppermute | solution.py:803
  72.1 47.6 %collective-permute-start.13 = (bf16[384,1024]{1,0:T(8,128)(2,1)S(1)}, bf16[384,1024]{1,0:T(8,128)(2,1)}, u32[]{:S(2)}, u32[]{:S(2)}) collective-permute-start(bf16[384,1024]{1,0:T(8,128)(2,1)S(1)} %pad_maximum_fusion.3.refs_8_.refs_4_), channel_id=1, source_target_pairs={{0,24},{4,28},{8,16},{12,20},{16,8},{20,12},{24,0},{28,4},{1,25},{... | collective-permute-start | bytes 2359304 | tf_op jit(solution)/shard_map/ppermute | solution.py:803
  73.5 46.6 %collective-permute-start.14 = (bf16[384,1024]{1,0:T(8,128)(2,1)S(1)}, bf16[384,1024]{1,0:T(8,128)(2,1)}, u32[]{:S(2)}, u32[]{:S(2)}) collective-permute-start(bf16[384,1024]{1,0:T(8,128)(2,1)S(1)} %pad_maximum_fusion.3.refs_8_.refs_4_), channel_id=1, source_target_pairs={{0,4},{4,0},{8,12},{12,8},{16,20},{20,16},{24,28},{28,24},{1,5},{5... | collective-permute-start | bytes 2359304 | tf_op jit(solution)/shard_map/ppermute | solution.py:803
  96.5 20.6 %collective-permute-start.4 = (bf16[1024,128]{1,0:T(8,128)(2,1)}, bf16[1024,128]{1,0:T(8,128)(2,1)S(1)}, u32[]{:S(2)}, u32[]{:S(2)}) collective-permute-start(bf16[1024,128]{1,0:T(8,128)(2,1)} %get-tuple-element.132.refs_0_), channel_id=1, source_target_pairs={{0,8},{4,12},{8,0},{12,4},{16,24},{20,28},{24,16},{28,20},{1,9},{5... | collective-permute-start | bytes 786440 | tf_op jit(solution)/shard_map/ppermute | solution.py:803
  96.8 20.4 %collective-permute-start.5 = (bf16[1024,128]{1,0:T(8,128)(2,1)}, bf16[1024,128]{1,0:T(8,128)(2,1)S(1)}, u32[]{:S(2)}, u32[]{:S(2)}) collective-permute-start(bf16[1024,128]{1,0:T(8,128)(2,1)} %get-tuple-element.132.refs_0_), channel_id=1, source_target_pairs={{0,16},{4,20},{8,24},{12,28},{16,0},{20,4},{24,8},{28,12},{1,17},{... | collective-permute-start | bytes 786440 | tf_op jit(solution)/shard_map/ppermute | solution.py:803
  189.2 25.4 %collective-permute-start.22 = (bf16[256,1024]{1,0:T(8,128)(2,1)}, bf16[256,1024]{1,0:T(8,128)(2,1)S(1)}, u32[]{:S(2)}, u32[]{:S(2)}) collective-permute-start(bf16[256,1024]{1,0:T(8,128)(2,1)} %get-tuple-element.143), channel_id=1, source_target_pairs={{0,16},{4,20},{8,24},{12,28},{16,0},{20,4},{24,8},{28,12},{1,17},{... | collective-permute-start | bytes 1572872 | tf_op jit(solution)/shard_map/ppermute | solution.py:803
  190.7 23.9 %collective-permute-start.23 = (bf16[256,1024]{1,0:T(8,128)(2,1)}, bf16[256,1024]{1,0:T(8,128)(2,1)S(1)}, u32[]{:S(2)}, u32[]{:S(2)}) collective-permute-start(bf16[256,1024]{1,0:T(8,128)(2,1)} %get-tuple-element.144), channel_id=1, source_target_pairs={{0,24},{4,28},{8,16},{12,20},{16,8},{20,12},{24,0},{28,4},{1,25},{... | collective-permute-start | bytes 1572872 | tf_op jit(solution)/shard_map/ppermute | solution.py:803
  229.1 115.9 %reduce-scatter.5.cloned.1.call-start = ((), (), s32[]{:S(2)}) async-start(), calls=%async_computation.9 | async-start | bytes 1310720 | tf_op jit(solution)/shard_map/reduce_scatter | solution.py:914
  238.9 30.3 %collective-permute-start.26 = (bf16[384,1024]{1,0:T(8,128)(2,1)}, bf16[384,1024]{1,0:T(8,128)(2,1)S(1)}, u32[]{:S(2)}, u32[]{:S(2)}) collective-permute-start(bf16[384,1024]{1,0:T(8,128)(2,1)} %get-tuple-element.166), channel_id=1, source_target_pairs={{0,8},{4,12},{8,0},{12,4},{16,24},{20,28},{24,16},{28,20},{1,9},{5... | collective-permute-start | bytes 2359304 | tf_op jit(solution)/shard_map/ppermute | solution.py:803
  239.4 36.3 %collective-permute-start.27 = (bf16[384,1024]{1,0:T(8,128)(2,1)}, bf16[384,1024]{1,0:T(8,128)(2,1)S(1)}, u32[]{:S(2)}, u32[]{:S(2)}) collective-permute-start(bf16[384,1024]{1,0:T(8,128)(2,1)} %get-tuple-element.167), channel_id=1, source_target_pairs={{0,16},{4,20},{8,24},{12,28},{16,0},{20,4},{24,8},{28,12},{1,17},{... | collective-permute-start | bytes 2359304 | tf_op jit(solution)/shard_map/ppermute | solution.py:803
  240.0 35.7 %collective-permute-start.28 = (bf16[384,1024]{1,0:T(8,128)(2,1)}, bf16[384,1024]{1,0:T(8,128)(2,1)S(1)}, u32[]{:S(2)}, u32[]{:S(2)}) collective-permute-start(bf16[384,1024]{1,0:T(8,128)(2,1)} %get-tuple-element.168), channel_id=1, source_target_pairs={{0,24},{4,28},{8,16},{12,20},{16,8},{20,12},{24,0},{28,4},{1,25},{... | collective-permute-start | bytes 2359304 | tf_op jit(solution)/shard_map/ppermute | solution.py:803
  308.7 46.4 %all-to-all-start.4 = ((bf16[32,40,384]{2,1,0:T(8,128)(2,1)}), bf16[32,40,384]{2,1,0:T(8,128)(2,1)S(1)}, u32[]{:S(2)}, u32[]{:S(2)}) async-start(bf16[32,40,384]{2,1,0:T(8,128)(2,1)} %pad_maximum_fusion.2), calls=%async_computation.5 | async-start | bytes 1966080 | tf_op jit(solution)/shard_map/all_to_all | solution.py:977
  315.1 29.9 %collective-permute-start.33 = (bf16[256,1024]{1,0:T(8,128)(2,1)}, bf16[256,1024]{1,0:T(8,128)(2,1)}, u32[]{:S(2)}, u32[]{:S(2)}) collective-permute-start(bf16[256,1024]{1,0:T(8,128)(2,1)} %get-tuple-element.193), channel_id=1, source_target_pairs={{0,24},{4,28},{8,16},{12,20},{16,8},{20,12},{24,0},{28,4},{1,25},{... | collective-permute-start | bytes 1572872 | tf_op jit(solution)/shard_map/ppermute | solution.py:803
  317.6 33.9 %collective-permute-start.31 = (bf16[256,1024]{1,0:T(8,128)(2,1)}, bf16[256,1024]{1,0:T(8,128)(2,1)}, u32[]{:S(2)}, u32[]{:S(2)}) collective-permute-start(bf16[256,1024]{1,0:T(8,128)(2,1)} %get-tuple-element.191), channel_id=1, source_target_pairs={{0,8},{4,12},{8,0},{12,4},{16,24},{20,28},{24,16},{28,20},{1,9},{5... | collective-permute-start | bytes 1572872 | tf_op jit(solution)/shard_map/ppermute | solution.py:803
  318.2 33.4 %collective-permute-start.32 = (bf16[256,1024]{1,0:T(8,128)(2,1)}, bf16[256,1024]{1,0:T(8,128)(2,1)}, u32[]{:S(2)}, u32[]{:S(2)}) collective-permute-start(bf16[256,1024]{1,0:T(8,128)(2,1)} %get-tuple-element.192), channel_id=1, source_target_pairs={{0,16},{4,20},{8,24},{12,28},{16,0},{20,4},{24,8},{28,12},{1,17},{... | collective-permute-start | bytes 1572872 | tf_op jit(solution)/shard_map/ppermute | solution.py:803
  323.3 21.0 %collective-permute-start.35 = (bf16[32,1024]{1,0:T(8,128)(2,1)S(1)}, bf16[32,1024]{1,0:T(8,128)(2,1)S(1)}, u32[]{:S(2)}, u32[]{:S(2)}) collective-permute-start(bf16[32,1024]{1,0:T(8,128)(2,1)S(1)} %get-tuple-element.219), channel_id=1, source_target_pairs={{0,2},{1,3},{2,0},{3,1},{4,6},{5,7},{6,4},{7,5},{8,10},{9,11},{10,... | collective-permute-start | bytes 196616 | tf_op jit(solution)/shard_map/ppermute | solution.py:952
  (72 other events, 547.0 us)
Sparse Core Ops, SparseCore 0:
  39.1 31.2 all-gather.3
  71.9 44.8 all-gather.5
  205.7 43.7 reduce-scatter.2
  286.9 26.9 reduce-scatter.4
